TPU v7x, 32 devices: a whole 2x2x4 slice. The times are simulated.
32 devices in a mesh: dp: 8 (over z, x), sub: 4 (over y, core).
Axes of the slice: x: 2, y: 2, z: 4, core: 2. Of those that a mesh axis runs over, the one named last changes fastest.
Arguments:
- tokens: bfloat16 [32768, 512], P(('dp', 'sub')), may hold values from -6 to 6
- cotangent: bfloat16 [32768, 512], P(('dp', 'sub')), may hold values from -6 to 6
- item_lengths: int32 [32, 8], P(('dp', 'sub')), may hold values from 0 to 1024, as said below
- joint_weight: bfloat16 [512, 1536], P(('dp', 'sub')), may hold values from -0.25 to 0.25
- output_weight: bfloat16 [512, 512], P(('dp', 'sub')), may hold values from -1.5 to 1.5
- expand_weight: bfloat16 [512, 2048], P(('dp', 'sub')), may hold values from -0.25 to 0.25
- reduce_weight: bfloat16 [2048, 512], P(('dp', 'sub')), may hold values from -0.125 to 0.125
- attn_gain: bfloat16 [512], P(('dp', 'sub')), may hold values from 0.099609375 to 1.8984375
- attn_shift: bfloat16 [512], P(('dp', 'sub')), may hold values from -3 to 3
- ffn_gain: bfloat16 [512], P(('dp', 'sub')), may hold values from 0.099609375 to 1.8984375
- ffn_shift: bfloat16 [512], P(('dp', 'sub')), may hold values from -3 to 3
- expand_bias: bfloat16 [2048], P(('dp', 'sub')), may hold values from -3 to 3
- reduce_bias: bfloat16 [512], P(('dp', 'sub')), may hold values from -3 to 3
Outputs:
- mixed: bfloat16 [32768, 512], P(('dp', 'sub'))
- token_grad: bfloat16 [32768, 512], P(('dp', 'sub'))
- joint_grad: float32 [512, 1536], P(('dp', 'sub'))
- output_grad: float32 [512, 512], P(('dp', 'sub'))
- expand_grad: float32 [512, 2048], P(('dp', 'sub'))
- reduce_grad: float32 [2048, 512], P(('dp', 'sub'))
- attn_gain_grad: float32 [512], P(('dp', 'sub'))
- attn_shift_grad: float32 [512], P(('dp', 'sub'))
- ffn_gain_grad: float32 [512], P(('dp', 'sub'))
- ffn_shift_grad: float32 [512], P(('dp', 'sub'))
- expand_bias_grad: float32 [2048], P(('dp', 'sub'))
- reduce_bias_grad: float32 [512], P(('dp', 'sub'))
Inputs may be any that keep to these rules, and one draw needn't show every extreme that they name: item_lengths[d, i] is the length of item i of device d, 0 for an empty slot; nonzero lengths are 64 or more; a device's items, each rounded up to a multiple of 16, fit in its 1024 slots; device 0's first item has 1024 tokens.
All inputs are finite; a program needn't handle non-finite values.
Results may differ from a plain program's by a relative error of at most 0.011.
Values may be sent and summed in bfloat16 or wider, within the bound.
No kernel may reach another device: no remote copies, remote signals or barrier semaphores. Data moves between devices by JAX's collectives and lax.ppermute only.
A program may use at most 256 MiB of HBM per device.

v0:
```python
import math

import jax
import jax.numpy as jnp
from jax import lax
from jax.sharding import PartitionSpec as P

D = 512
HEADS = 8
BLOCK = 16
LEVELS = 7


LOG_TWO = math.log(2.0)
NEGATIVE = -1e30
ROOT_HALF = 1.0 / math.sqrt(2.0)
DENSITY = 1.0 / math.sqrt(2.0 * math.pi)


def token_ids(lengths, seq_len):
    padded = (lengths + BLOCK - 1) // BLOCK * BLOCK
    ends = jnp.cumsum(padded)
    starts = ends - padded
    position = jnp.arange(seq_len, dtype=jnp.int32)
    inside = (position[:, None] >= starts[None, :]) & (
        position[:, None] < (starts + lengths)[None, :]
    )
    live = jnp.any(inside, axis=1)
    number = jnp.arange(lengths.shape[0], dtype=jnp.int32)
    item = jnp.sum(jnp.where(inside, number[None, :], 0), axis=1)
    segment = jnp.where(live, item, -1 - position)
    return (live.astype(jnp.float32), segment)


def level_mask(segment, seq_len, level):
    factor = 2**level
    width = BLOCK * factor
    blocks = seq_len // width
    grouped = segment.reshape(seq_len // factor, factor)
    smallest = jnp.min(grouped, axis=1)
    largest = jnp.max(grouped, axis=1)
    absent = -3 * seq_len
    coarse_id = jnp.where(smallest == largest, smallest, absent).reshape(blocks, BLOCK)
    padded = jnp.pad(coarse_id, ((1, 1), (0, 0)), constant_values=absent)
    window = jnp.concatenate([padded[:-2], padded[1:-1], padded[2:]], axis=1)
    valid = window[:, None, :] == segment.reshape(blocks, width)[:, :, None]
    if level > 0:
        half = width // 2
        position = jnp.arange(seq_len, dtype=jnp.int32).reshape(blocks, width)
        lower = (position // half - 1) * half
        start = (
            (jnp.arange(blocks, dtype=jnp.int32)[:, None] - 1) * BLOCK
            + jnp.arange(3 * BLOCK, dtype=jnp.int32)[None, :]
        ) * factor
        covered = (start[:, None, :] >= lower[:, :, None]) & (
            start[:, None, :] < lower[:, :, None] + 3 * half
        )
        valid = valid & jnp.logical_not(covered)
    return valid


def windows(coarse_values, blocks):
    heads, dim = (coarse_values.shape[1], coarse_values.shape[2])
    grouped = coarse_values.reshape(blocks, BLOCK, heads, dim)
    padded = jnp.pad(grouped, ((1, 1), (0, 0), (0, 0), (0, 0)))
    return jnp.concatenate([padded[:-2], padded[1:-1], padded[2:]], axis=1)


def unwindow(window_grad, blocks):
    heads, dim = (window_grad.shape[2], window_grad.shape[3])
    edges = ((0, 0), (0, 0), (0, 0))
    total = (
        jnp.pad(window_grad[:, :BLOCK], ((0, 2),) + edges)
        + jnp.pad(window_grad[:, BLOCK : 2 * BLOCK], ((1, 1),) + edges)
        + jnp.pad(window_grad[:, 2 * BLOCK :], ((2, 0),) + edges)
    )
    return total[1 : blocks + 1].reshape(blocks * BLOCK, heads, dim)


def coarse(values, factor):
    if factor == 1:
        return values
    seq_len, heads, dim = values.shape
    grouped = values.reshape(seq_len // factor, factor, heads, dim).astype(jnp.float32)
    return jnp.mean(grouped, axis=1).astype(jnp.bfloat16)


def spread_out(grad, factor):
    if factor == 1:
        return grad
    return jnp.repeat(grad, factor, axis=0) / factor


def to_rows(reduced):
    return reduced.transpose(0, 2, 1).reshape(-1, reduced.shape[1])


def from_rows(rows, blocks, width):
    return rows.reshape(blocks, width, -1).transpose(0, 2, 1)[..., None]


def attend(query, keys, values, segment, log_total):
    seq_len, heads, dim = query.shape
    factor_scale = dim ** (-0.5)
    scores = []
    key_windows = []
    value_windows = []
    for level in range(LEVELS):
        factor = 2**level
        width = BLOCK * factor
        blocks = seq_len // width
        valid = level_mask(segment, seq_len, level)
        key_window = windows(coarse(keys, factor), blocks)
        value_window = windows(coarse(values, factor), blocks)
        raw = jnp.einsum(
            "bwhd,bjhd->bhwj",
            query.reshape(blocks, width, heads, dim),
            key_window,
            preferred_element_type=jnp.float32,
        )
        scores.append(jnp.where(valid[:, None], raw * factor_scale + level * LOG_TWO, NEGATIVE))
        key_windows.append(key_window)
        value_windows.append(value_window)
    if log_total is None:
        peak = to_rows(jnp.max(scores[0], axis=-1))
        for score in scores[1:]:
            peak = jnp.maximum(peak, to_rows(jnp.max(score, axis=-1)))
        total = jnp.zeros((seq_len, heads), jnp.float32)
        for score in scores:
            blocks, width = (score.shape[0], score.shape[2])
            total = total + to_rows(
                jnp.sum(jnp.exp(score - from_rows(peak, blocks, width)), axis=-1)
            )
        log_total = peak + jnp.log(total)
    probs = []
    context = jnp.zeros((seq_len, heads, dim), jnp.float32)
    for level in range(LEVELS):
        score = scores[level]
        blocks, width = (score.shape[0], score.shape[2])
        weight = jnp.exp(score - from_rows(log_total, blocks, width))
        probs.append(weight)
        part = jnp.einsum(
            "bhwj,bjhd->bwhd",
            weight.astype(jnp.bfloat16),
            value_windows[level],
            preferred_element_type=jnp.float32,
        )
        context = context + part.reshape(seq_len, heads, dim)
    return (context.reshape(seq_len, heads * dim), log_total, probs, key_windows, value_windows)


def attend_back(query, context_grad, probs, key_windows, value_windows):
    seq_len, heads, dim = query.shape
    factor_scale = dim ** (-0.5)
    prob_grads = []
    inner = jnp.zeros((seq_len, heads), jnp.float32)
    for level in range(LEVELS):
        width = BLOCK * 2**level
        blocks = seq_len // width
        grad_block = context_grad.reshape(blocks, width, heads, dim)
        prob_grad = jnp.einsum(
            "bwhd,bjhd->bhwj", grad_block, value_windows[level], preferred_element_type=jnp.float32
        )
        inner = inner + to_rows(jnp.sum(probs[level] * prob_grad, axis=-1))
        prob_grads.append(prob_grad)
    query_grad = jnp.zeros((seq_len, heads, dim), jnp.float32)
    key_grad = jnp.zeros((seq_len, heads, dim), jnp.float32)
    value_grad = jnp.zeros((seq_len, heads, dim), jnp.float32)
    for level in range(LEVELS):
        factor = 2**level
        width = BLOCK * factor
        blocks = seq_len // width
        weight = probs[level]
        grad_block = context_grad.reshape(blocks, width, heads, dim)
        query_block = query.reshape(blocks, width, heads, dim)
        score_grad = (weight * (prob_grads[level] - from_rows(inner, blocks, width))).astype(
            jnp.bfloat16
        )
        query_part = jnp.einsum(
            "bhwj,bjhd->bwhd", score_grad, key_windows[level], preferred_element_type=jnp.float32
        )
        query_grad = query_grad + query_part.reshape(seq_len, heads, dim) * factor_scale
        key_part = (
            jnp.einsum(
                "bhwj,bwhd->bjhd", score_grad, query_block, preferred_element_type=jnp.float32
            )
            * factor_scale
        )
        value_part = jnp.einsum(
            "bhwj,bwhd->bjhd",
            weight.astype(jnp.bfloat16),
            grad_block,
            preferred_element_type=jnp.float32,
        )
        key_grad = key_grad + spread_out(unwindow(key_part, blocks), factor)
        value_grad = value_grad + spread_out(unwindow(value_part, blocks), factor)
    return jnp.concatenate(
        [
            query_grad.reshape(seq_len, heads * dim),
            key_grad.reshape(seq_len, heads * dim),
            value_grad.reshape(seq_len, heads * dim),
        ],
        axis=1,
    )


def normalize(values):
    centre = values - jnp.mean(values, axis=-1, keepdims=True)
    scale = lax.rsqrt(jnp.mean(centre * centre, axis=-1, keepdims=True) + 1e-05)
    return (centre * scale, scale)


def norm_back(grad, normed, scale, gain):
    scaled = grad * gain
    return scale * (
        scaled
        - jnp.mean(scaled, axis=-1, keepdims=True)
        - normed * jnp.mean(scaled * normed, axis=-1, keepdims=True)
    )


def contract_rows(left, right):
    return lax.dot_general(
        left, right, (((0,), (0,)), ((), ())), preferred_element_type=jnp.float32
    )


def contract_cols(left, right):
    return lax.dot_general(
        left, right, (((1,), (1,)), ((), ())), preferred_element_type=jnp.float32
    )


def recompute(values, live, segment, weights, log_total):
    (
        joint,
        output_w,
        expand,
        reduce_w,
        attn_gain,
        attn_shift,
        ffn_gain,
        ffn_shift,
        expand_bias,
        reduce_bias,
    ) = weights
    seq_len = values.shape[0]
    first_hat, first_scale = normalize(values)
    first_in = (first_hat * attn_gain.astype(jnp.float32) + attn_shift.astype(jnp.float32)).astype(
        jnp.bfloat16
    )
    joint_out = jnp.dot(first_in, joint, preferred_element_type=jnp.float32).astype(jnp.bfloat16)
    query = joint_out[:, :D].reshape(seq_len, HEADS, D // HEADS)
    keys = joint_out[:, D : 2 * D].reshape(seq_len, HEADS, D // HEADS)
    vals = joint_out[:, 2 * D :].reshape(seq_len, HEADS, D // HEADS)
    context, log_total, probs, key_windows, value_windows = attend(
        query, keys, vals, segment, log_total
    )
    context_low = context.astype(jnp.bfloat16)
    hidden = (
        values + jnp.dot(context_low, output_w, preferred_element_type=jnp.float32) * live[:, None]
    )
    second_hat, second_scale = normalize(hidden)
    second_in = (second_hat * ffn_gain.astype(jnp.float32) + ffn_shift.astype(jnp.float32)).astype(
        jnp.bfloat16
    )
    expanded = jnp.dot(second_in, expand, preferred_element_type=jnp.float32) + expand_bias.astype(
        jnp.float32
    )
    activated = jax.nn.gelu(expanded, approximate=False).astype(jnp.bfloat16)
    reduced = jnp.dot(activated, reduce_w, preferred_element_type=jnp.float32) + reduce_bias.astype(
        jnp.float32
    )
    return {
        "mixed": hidden + reduced * live[:, None],
        "log_total": log_total,
        "first_hat": first_hat,
        "first_scale": first_scale,
        "first_in": first_in,
        "query": query,
        "probs": probs,
        "key_windows": key_windows,
        "value_windows": value_windows,
        "context_low": context_low,
        "second_hat": second_hat,
        "second_scale": second_scale,
        "second_in": second_in,
        "expanded": expanded,
        "activated": activated,
    }


def fetch_forward(
    joint,
    output_w,
    expand,
    reduce_w,
    attn_gain,
    attn_shift,
    ffn_gain,
    ffn_shift,
    expand_bias,
    reduce_bias,
):
    return (
        lax.all_gather(joint, ("dp", "sub"), axis=0, tiled=True),
        lax.all_gather(output_w, ("dp", "sub"), axis=0, tiled=True),
        lax.all_gather(expand, ("dp", "sub"), axis=0, tiled=True),
        lax.all_gather(reduce_w, ("dp", "sub"), axis=0, tiled=True),
        lax.all_gather(attn_gain, ("dp", "sub"), axis=0, tiled=True),
        lax.all_gather(attn_shift, ("dp", "sub"), axis=0, tiled=True),
        lax.all_gather(ffn_gain, ("dp", "sub"), axis=0, tiled=True),
        lax.all_gather(ffn_shift, ("dp", "sub"), axis=0, tiled=True),
        lax.all_gather(expand_bias, ("dp", "sub"), axis=0, tiled=True),
        lax.all_gather(reduce_bias, ("dp", "sub"), axis=0, tiled=True),
    )


def fetch_backward(
    joint,
    output_w,
    expand,
    reduce_w,
    attn_gain,
    attn_shift,
    ffn_gain,
    ffn_shift,
    expand_bias,
    reduce_bias,
):
    return (
        lax.all_gather(joint, ("dp", "sub"), axis=0, tiled=True),
        lax.all_gather(output_w, ("dp", "sub"), axis=0, tiled=True),
        lax.all_gather(expand, ("dp", "sub"), axis=0, tiled=True),
        lax.all_gather(reduce_w, ("dp", "sub"), axis=0, tiled=True),
        lax.all_gather(attn_gain, ("dp", "sub"), axis=0, tiled=True),
        lax.all_gather(attn_shift, ("dp", "sub"), axis=0, tiled=True),
        lax.all_gather(ffn_gain, ("dp", "sub"), axis=0, tiled=True),
        lax.all_gather(ffn_shift, ("dp", "sub"), axis=0, tiled=True),
        lax.all_gather(expand_bias, ("dp", "sub"), axis=0, tiled=True),
        lax.all_gather(reduce_bias, ("dp", "sub"), axis=0, tiled=True),
    )


def return_grads(
    joint,
    output_w,
    expand,
    reduce_w,
    attn_gain,
    attn_shift,
    ffn_gain,
    ffn_shift,
    expand_bias,
    reduce_bias,
):
    return (
        lax.psum_scatter(joint, ("dp", "sub"), scatter_dimension=0, tiled=True),
        lax.psum_scatter(output_w, ("dp", "sub"), scatter_dimension=0, tiled=True),
        lax.psum_scatter(expand, ("dp", "sub"), scatter_dimension=0, tiled=True),
        lax.psum_scatter(reduce_w, ("dp", "sub"), scatter_dimension=0, tiled=True),
        lax.psum_scatter(attn_gain, ("dp", "sub"), scatter_dimension=0, tiled=True),
        lax.psum_scatter(attn_shift, ("dp", "sub"), scatter_dimension=0, tiled=True),
        lax.psum_scatter(ffn_gain, ("dp", "sub"), scatter_dimension=0, tiled=True),
        lax.psum_scatter(ffn_shift, ("dp", "sub"), scatter_dimension=0, tiled=True),
        lax.psum_scatter(expand_bias, ("dp", "sub"), scatter_dimension=0, tiled=True),
        lax.psum_scatter(reduce_bias, ("dp", "sub"), scatter_dimension=0, tiled=True),
    )


def shards(
    tokens,
    cotangent,
    item_lengths,
    joint_weight,
    output_weight,
    expand_weight,
    reduce_weight,
    attn_gain,
    attn_shift,
    ffn_gain,
    ffn_shift,
    expand_bias,
    reduce_bias,
):
    seq_len = tokens.shape[0]
    live, segment = token_ids(item_lengths[0], seq_len)
    values = tokens.astype(jnp.float32)
    weights = fetch_forward(
        joint_weight,
        output_weight,
        expand_weight,
        reduce_weight,
        attn_gain,
        attn_shift,
        ffn_gain,
        ffn_shift,
        expand_bias,
        reduce_bias,
    )
    first_state = recompute(values, live, segment, weights, None)
    mixed = first_state["mixed"].astype(jnp.bfloat16)
    again = fetch_backward(
        joint_weight,
        output_weight,
        expand_weight,
        reduce_weight,
        attn_gain,
        attn_shift,
        ffn_gain,
        ffn_shift,
        expand_bias,
        reduce_bias,
    )
    state = recompute(values, live, segment, again, first_state["log_total"])
    (
        joint,
        output_w,
        expand,
        reduce_w,
        gain_first,
        shift_first,
        gain_second,
        shift_second,
        bias_expand,
        bias_reduce,
    ) = again
    live_column = live[:, None]
    upstream = cotangent.astype(jnp.float32)
    out_grad = (upstream * live_column).astype(jnp.bfloat16)
    reduce_bias_grad = jnp.sum(out_grad.astype(jnp.float32), axis=0)
    reduce_grad = contract_rows(state["activated"], out_grad)
    activated_grad = contract_cols(out_grad, reduce_w)
    expanded = state["expanded"]
    slope = (
        0.5 * (1.0 + lax.erf(expanded * ROOT_HALF))
        + expanded * jnp.exp(-0.5 * expanded * expanded) * DENSITY
    )
    expanded_grad = (activated_grad * slope).astype(jnp.bfloat16)
    expand_bias_grad = jnp.sum(expanded_grad.astype(jnp.float32), axis=0)
    expand_grad = contract_rows(state["second_in"], expanded_grad)
    second_in_grad = contract_cols(expanded_grad, expand)
    ffn_gain_grad = jnp.sum(second_in_grad * state["second_hat"], axis=0)
    ffn_shift_grad = jnp.sum(second_in_grad, axis=0)
    hidden_grad = upstream + norm_back(
        second_in_grad, state["second_hat"], state["second_scale"], gain_second.astype(jnp.float32)
    )
    branch_grad = (hidden_grad * live_column).astype(jnp.bfloat16)
    output_grad = contract_rows(state["context_low"], branch_grad)
    context_grad = contract_cols(branch_grad, output_w).astype(jnp.bfloat16)
    query = state["query"]
    joint_out_grad = attend_back(
        query,
        context_grad.reshape(query.shape),
        state["probs"],
        state["key_windows"],
        state["value_windows"],
    ).astype(jnp.bfloat16)
    joint_grad = contract_rows(state["first_in"], joint_out_grad)
    first_in_grad = contract_cols(joint_out_grad, joint)
    attn_gain_grad = jnp.sum(first_in_grad * state["first_hat"], axis=0)
    attn_shift_grad = jnp.sum(first_in_grad, axis=0)
    token_grad = (
        hidden_grad
        + norm_back(
            first_in_grad, state["first_hat"], state["first_scale"], gain_first.astype(jnp.float32)
        )
    ).astype(jnp.bfloat16)
    summed = return_grads(
        joint_grad,
        output_grad,
        expand_grad,
        reduce_grad,
        attn_gain_grad,
        attn_shift_grad,
        ffn_gain_grad,
        ffn_shift_grad,
        expand_bias_grad,
        reduce_bias_grad,
    )
    return (
        mixed,
        token_grad,
        summed[0],
        summed[1],
        summed[2],
        summed[3],
        summed[4],
        summed[5],
        summed[6],
        summed[7],
        summed[8],
        summed[9],
    )


def solution(mesh):
    placed = (
        P(("dp", "sub"), None),
        P(("dp", "sub"), None),
        P(("dp", "sub"), None),
        P(("dp", "sub"), None),
        P(("dp", "sub"), None),
        P(("dp", "sub"), None),
        P(("dp", "sub"), None),
        P(("dp", "sub")),
        P(("dp", "sub")),
        P(("dp", "sub")),
        P(("dp", "sub")),
        P(("dp", "sub")),
        P(("dp", "sub")),
    )
    return jax.shard_map(
        shards,
        mesh=mesh,
        in_specs=placed,
        out_specs=(
            P(("dp", "sub"), None),
            P(("dp", "sub"), None),
            P(("dp", "sub"), None),
            P(("dp", "sub"), None),
            P(("dp", "sub"), None),
            P(("dp", "sub"), None),
            P(("dp", "sub")),
            P(("dp", "sub")),
            P(("dp", "sub")),
            P(("dp", "sub")),
            P(("dp", "sub")),
            P(("dp", "sub")),
        ),
        check_vma=False,
    )
```

profile of v0, /device:TPU:0, one launch (start us, length us, event | category | flops | bytes accessed | tf_op | source)
XLA Modules:
  0.0 1387.1 jit_solution(7859154605554907455)
XLA Ops:
  22.1 42.5 %all-reduce.73 = (bf16[512]{0:T(512)(128)(2,1)S(1)}, bf16[512]{0:T(512)(128)(2,1)S(1)}, bf16[512]{0:T(512)(128)(2,1)S(1)}, bf16[512]{0:T(512)(128)(2,1)S(1)}, bf...) all-reduce(bf16[512]{0:T(512)(128)(2,1)S(1)} %dynamic-update-slice.1, ...), channel_id=1, replica_groups=mesh['dp'=8,'sub'=4] {'dp','sub'}, use_global_device_ids=true, to_apply=%add.61 | all-reduce | flops 4608 | bytes 18432
  68.9 44.9 %all_gather.42 = bf16[512,512]{1,0:T(8,128)(2,1)} all-gather(bf16[16,512]{1,0:T(8,128)(2,1)S(1)} %copy-done.270), channel_id=1, replica_groups=mesh['dp'=8,'sub'=4] {'dp','sub'}, dimensions={0}, use_global_device_ids=true | all-gather | bytes 540672 | tf_op jit(solution)/shard_map/all_gather | solution.py:307
  476.4 6.9 add_convert_fusion.4
  486.5 25.1 %fusion.2 = (bf16[1024,2048]{1,0:T(8,128)(2,1)}, f32[1024,2048]{1,0:T(8,128)}) fusion(f32[2048]{0:T(1024)S(1)} %convert_element_type.488, bf16[512,2048]{1,0:T(8,128)(2,1)} %all-gather.6.cloned.1.call-done, f32[1024,512]{0,1:T(8,128)} %copy-done.17, f32[512]{0:T(512)} %convert_element_type.486, f32[512]{0:T(512)} %convert_element_type.485, ...), kind=kOutput, calls=%fused_computation.5 | convolution fusion | flops 2288517120 | bytes 16797696 | tf_op jit(solution)/shard_map/dot_general | solution.py:267
  511.5 8.9 convert_reduce_fusion
  594.8 8.6 multiply_reduce_fusion.1
  610.6 6.1 multiply_reduce_fusion
  641.4 8.5 convolution_bitcast_fusion.1
  689.2 7.5 convolution_bitcast_fusion
  710.3 6.0 multiply_convert_fusion.1
  752.2 8.0 copy.898
  787.8 6.0 fusion.284
  809.5 10.0 fusion.283
  819.5 10.0 fusion.282
  956.6 6.2 copy.953
  967.5 6.0 pad_add_fusion.2
  982.6 7.0 add_convert_fusion
  999.3 6.7 fusion.81
  1007.7 6.8 fusion.277
  1015.2 6.3 add_convert_fusion.2
  1032.7 38.0 %all-reduce.72 = (f32[512]{0:T(512)S(1)}, f32[512]{0:T(512)S(1)}, f32[512]{0:T(512)S(1)}, f32[512]{0:T(512)S(1)}, f32[2048]{0:T(1024)S(1)}, /*index=5*/f32[512]{0:T(512)S(1)}) all-reduce(f32[512]{0:T(512)S(1)} %get-tuple-element.74, f32[512]{0:T(512)S(1)} %get-tuple-element.224, ...), channel_id=6, replica_groups=mesh['dp'=8,'sub'=4] {'dp','sub'}, use_global_device_ids=true, to_apply=%region_61.62.clone | all-reduce | flops 4608 | bytes 36864
  1079.8 16.3 %reduce-scatter.5.cloned.1.call-done = f32[16,1536]{1,0:T(8,128)} async-done(((f32[512,1536]{1,0:T(8,128)}), f32[16,1536]{1,0:T(8,128)}) %reduce-scatter.5.cloned.1.call-update) | async-done | bytes 98320 | tf_op jit(solution)/shard_map/reduce_scatter | solution.py:358
  1096.1 143.7 %reduce-scatter.11.cloned.1.call-done = f32[64,512]{1,0:T(8,128)} async-done(((f32[2048,512]{1,0:T(8,128)}), f32[64,512]{1,0:T(8,128)}) %reduce-scatter.11.cloned.1.call-update) | async-done | bytes 131088 | tf_op jit(solution)/shard_map/reduce_scatter | solution.py:361
  1239.8 140.2 %reduce-scatter.9.cloned.1.call-done = f32[16,2048]{1,0:T(8,128)} async-done(((f32[512,2048]{1,0:T(8,128)}), f32[16,2048]{1,0:T(8,128)}) %reduce-scatter.9.cloned.1.call-update) | async-done | bytes 131088 | tf_op jit(solution)/shard_map/reduce_scatter | solution.py:360
  (1107 shorter events, 793.5 us)
Async XLA Ops:
  7.2 61.7 %copy-start.270 = (bf16[16,512]{1,0:T(8,128)(2,1)S(1)}, bf16[16,512]{1,0:T(8,128)(2,1)}, u32[]{:S(2)}) copy-start(bf16[16,512]{1,0:T(8,128)(2,1)} %param.17) | copy-start | bytes 49156
  7.2 106.6 %copy-start.158 = (bf16[1024,512]{1,0:T(8,128)(2,1)S(1)}, bf16[1024,512]{1,0:T(8,128)(2,1)}, u32[]{:S(2)}) copy-start(bf16[1024,512]{1,0:T(8,128)(2,1)} %param.13) | copy-start | bytes 3145732
  7.2 115.1 %all-gather.4.cloned.1.call-start = ((), (), s32[]{:S(2)}) async-start(), calls=%async_computation.4 | async-start | bytes 1622016 | tf_op jit(solution)/shard_map/all_gather | solution.py:306
  7.9 478.5 %all-gather.6.cloned.1.call-start = ((), (), s32[]{:S(2)}) async-start(), calls=%async_computation.5 | async-start | bytes 2162688 | tf_op jit(solution)/shard_map/all_gather | solution.py:308
  8.7 502.8 %all-gather.8.cloned.1.call-start = ((), (), s32[]{:S(2)}) async-start(), calls=%async_computation.6 | async-start | bytes 2162688 | tf_op jit(solution)/shard_map/all_gather | solution.py:309
  9.4 1070.4 %reduce-scatter.7.cloned.1.call-start = ((), (), s32[]{:S(2)}) async-start(), calls=%async_computation.8 | async-start | bytes 1081344 | tf_op jit(solution)/shard_map/reduce_scatter | solution.py:359
  65.2 57.1 %copy-start.268 = (f32[512]{0:T(512)}, f32[512]{0:T(512)S(1)}, u32[]{:S(2)}) copy-start(f32[512]{0:T(512)S(1)} %convert_element_type.426) | copy-start | bytes 6148
  68.1 254.7 %copy-start.97 = (pred[64,16,48]{2,1,0:T(8,128)(4,1)}, pred[64,16,48]{2,1,0:T(8,128)(4,1)S(1)}, u32[]{:S(2)}) copy-start(pred[64,16,48]{2,1,0:T(8,128)(4,1)S(1)} %broadcast_compare_fusion) | copy-start | bytes 147460
  129.9 58.8 %copy-start.9 = (bf16[1024,512]{0,1:T(8,128)(2,1)}, bf16[1024,512]{0,1:T(8,128)(2,1)S(1)}, u32[]{:S(2)}) copy-start(bf16[1024,512]{0,1:T(8,128)(2,1)S(1)} %copy.720) | copy-start | bytes 3145732
  292.7 13.0 copy-start.132
  298.9 13.5 copy-start.136
  305.7 16.2 %copy-start.111 = (f32[8,1024]{1,0:T(8,128)}, f32[8,1024]{1,0:T(8,128)S(1)}, u32[]{:S(2)}) copy-start(f32[8,1024]{1,0:T(8,128)S(1)} %exponential_reduce_fusion.3) | copy-start | bytes 98308
  334.1 61.2 %copy-start.107 = (bf16[4,16,8,64]{3,1,2,0:T(8,128)(2,1)}, bf16[4,16,8,64]{3,1,2,0:T(8,128)(2,1)S(1)}, u32[]{:S(2)}) copy-start(bf16[4,16,8,64]{3,1,2,0:T(8,128)(2,1)S(1)} %copy.837) | copy-start | bytes 196612
  484.8 46.5 %copy-start.258 = (f32[1024]{0:T(1024)}, f32[1024]{0:T(1024)S(1)}, u32[]{:S(2)}) copy-start(f32[1024]{0:T(1024)S(1)} %broadcast_multiply_fusion.4) | copy-start | bytes 12292
  486.4 44.8 %copy-start.264 = (f32[1024]{0:T(1024)}, f32[1024]{0:T(1024)S(1)}, u32[]{:S(2)}) copy-start(f32[1024]{0:T(1024)S(1)} %add_rsqrt_fusion) | copy-start | bytes 12292
  725.4 370.7 %reduce-scatter.5.cloned.1.call-start = ((), (), s32[]{:S(2)}) async-start(), calls=%async_computation.7 | async-start | bytes 3244032 | tf_op jit(solution)/shard_map/reduce_scatter | solution.py:358
  819.5 13.2 copy-start.163
  819.5 13.2 copy-start.164
  819.5 14.0 %copy-start.119 = (f32[8,16,8,64]{3,1,2,0:T(8,128)S(1)}, f32[8,16,8,64]{3,1,2,0:T(8,128)}, u32[]{:S(2)}) copy-start(f32[8,16,8,64]{3,1,2,0:T(8,128)} %get-tuple-element.135) | copy-start | bytes 786436
  819.5 14.0 %copy-start.120 = (f32[8,16,8,64]{3,1,2,0:T(8,128)S(1)}, f32[8,16,8,64]{3,1,2,0:T(8,128)}, u32[]{:S(2)}) copy-start(f32[8,16,8,64]{3,1,2,0:T(8,128)} %get-tuple-element.136) | copy-start | bytes 786436
  819.5 14.0 %copy-start.121 = (f32[8,16,8,64]{3,1,2,0:T(8,128)S(1)}, f32[8,16,8,64]{3,1,2,0:T(8,128)}, u32[]{:S(2)}) copy-start(f32[8,16,8,64]{3,1,2,0:T(8,128)} %get-tuple-element.137) | copy-start | bytes 786436
  998.2 241.6 %reduce-scatter.11.cloned.1.call-start = ((), (), s32[]{:S(2)}) async-start(), calls=%async_computation.10 | async-start | bytes 4325376 | tf_op jit(solution)/shard_map/reduce_scatter | solution.py:361
  1006.1 373.9 %reduce-scatter.9.cloned.1.call-start = ((), (), s32[]{:S(2)}) async-start(), calls=%async_computation.9 | async-start | bytes 4325376 | tf_op jit(solution)/shard_map/reduce_scatter | solution.py:360
  1030.1 43.5 %copy-start.16 = (f32[1024,512]{0,1:T(8,128)S(1)}, f32[1024,512]{0,1:T(8,128)}, u32[]{:S(2)}) copy-start(f32[1024,512]{0,1:T(8,128)} %copy-done.15) | copy-start | bytes 6291460
  (275 other events, 1019.4 us)
Sparse Core Ops, SparseCore 0:
  10.9 58.0 all-gather.3
  71.9 55.5 all-gather.5
  130.3 55.2 all-gather.7
  725.5 130.8 reduce-scatter.6
  998.3 97.7 reduce-scatter.4
  1098.9 140.8 reduce-scatter.10
  1242.7 137.2 reduce-scatter.8
where the time goes:
time: 1400 us; the launch traced here: 1390 us
  local copies, waits for them, and re-layouts  561 us (40%)
  waiting for transfers between devices  302 us (22%)
  matrix products  212 us (15%)
  other arithmetic  169 us (12%)
  blocking collectives  125 us (9%)
  between operations  17.5 us (1%)
    reduce_scatter x1, waiting for transfers between devices, return_grads(): lax.psum_scatter(reduce_w, ('dp', 'sub'), scatter_dimension=0, tiled=True)  144 us
    reduce_scatter x1, waiting for transfers between devices, return_grads(): lax.psum_scatter(expand, ('dp', 'sub'), scatter_dimension=0, tiled=True)  140 us
    reshape x108, local copies, waits for them, and re-layouts, to_rows(): return reduced.transpose(0, 2, 1).reshape(-1, reduced.shape[1])  105 us
    unnamed x2, blocking collectives  80.5 us
    div x24, local copies, waits for them, and re-layouts, spread_out(): return jnp.repeat(grad, factor, axis=0) / factor  66.6 us
    unnamed x608, local copies, waits for them, and re-layouts  54 us
    all_gather x1, blocking collectives, fetch_forward(): lax.all_gather(output_w, ('dp', 'sub'), axis=0, tiled=True)  44.9 us
    reshape x10, local copies, waits for them, and re-layouts, attend(): context = context + part.reshape(seq_len, heads, dim)  44.1 us
  transfers between devices with their start and end apart: 7, of which 3 were waited for; matrix products, arithmetic and copies ran while one was open for 51% of the time, Pallas kernels for 0%

commit v1 on v0

v1 whole, which is shorter than its diff:
```python
import functools
import math

import jax
import jax.numpy as jnp
import numpy as np
from jax import lax
from jax.experimental import pallas as pl
from jax.experimental.pallas import tpu as pltpu
from jax.sharding import PartitionSpec as P

HEADS = 8
BLOCK = 16
LEVELS = 7
TILE = 128
GROUPS = 2
LOG_TWO = math.log(2.0)
NEGATIVE = -1e30
ROOT_HALF = 1.0 / math.sqrt(2.0)
DENSITY = 1.0 / math.sqrt(2.0 * math.pi)
AXES = ("dp", "sub")
BF = jnp.bfloat16
F32 = jnp.float32
MIB = 1 << 20


class Level:
    def __init__(self, level, seq, base):
        self.level = level
        self.factor = 1 << level
        self.count = seq // self.factor
        self.width = BLOCK * self.factor
        self.blocks = seq // self.width
        self.pad = BLOCK if self.blocks > 2 else 0
        self.base = base
        self.rows = self.count + 2 * self.pad
        if self.width <= TILE:
            self.window = TILE // self.factor + 2 * BLOCK
        else:
            self.window = min(3, self.blocks) * BLOCK

    def first(self, tile):
        if self.width <= TILE:
            return tile * (TILE // self.factor)
        if self.blocks > 2:
            return (tile // (self.width // TILE)) * BLOCK
        return 0

    def row(self, tile):
        first = self.first(tile)
        return pl.multiple_of(self.base + first, BLOCK) if not isinstance(first, int) else self.base + first


def geometry(seq):
    levels, base = [], 0
    for level in range(LEVELS):
        levels.append(Level(level, seq, base))
        base += levels[-1].rows
    return levels, base, sum(v.window for v in levels)


def pooling(seq):
    levels, total, _ = geometry(seq)
    near = [v for v in levels[1:] if v.width <= TILE]
    far = [v for v in levels[1:] if v.width > TILE]
    near_rows = sum(TILE // v.factor for v in near)
    fine = np.zeros((near_rows, TILE), np.float32)
    row = 0
    for v in near:
        for j in range(TILE // v.factor):
            fine[row, j * v.factor : (j + 1) * v.factor] = 1.0 / v.factor
            row += 1
    far_base = far[0].base
    wide = np.zeros((total - far_base, seq), np.float32)
    for v in far:
        for j in range(v.count):
            wide[v.base - far_base + v.pad + j, j * v.factor : (j + 1) * v.factor] = 1.0 / v.factor
    spread = np.zeros((seq, near_rows + total - far_base), np.float32)
    for t in range(seq // TILE):
        spread[t * TILE : (t + 1) * TILE, :near_rows] = fine.T
    spread[:, near_rows:] = wide.T
    return near, far_base, fine, wide, spread


class Order:
    def __init__(self, devices):
        self.devices = devices
        self.bits = [1 << k for k in reversed(range(devices.bit_length() - 1))]
        self.stepped = devices == 32

    def flip(self, p):
        value = 0
        for k, bit in enumerate(self.bits):
            value = value + ((p >> k) & 1) * bit
        return value


def dot(left, right, contract=(1, 0)):
    return lax.dot_general(
        left, right, (((contract[0],), (contract[1],)), ((), ())), preferred_element_type=F32
    )


def iota(shape, axis):
    return lax.broadcasted_iota(jnp.int32, shape, axis)


def unpack_rows(order, me, source, columns, target, chunk):
    if not order.stepped:
        target[...] = source[:, columns]
        return
    for p in range(order.devices):
        row = pl.multiple_of((me ^ order.flip(p)) * chunk, chunk)
        target[pl.ds(row, chunk), :] = source[p * chunk : (p + 1) * chunk, columns]


def pack_rows(order, me, value, target, columns, chunk, scratch):
    if not order.stepped:
        target[:, columns] = value
        return
    scratch[...] = value
    for p in range(order.devices):
        row = pl.multiple_of((me ^ order.flip(p)) * chunk, chunk)
        target[p * chunk : (p + 1) * chunk, columns] = scratch[pl.ds(row, chunk), :]


def owners(order, me, shape):
    return me ^ order.flip(iota(shape, 0))


def spread_lanes(order, me, block, row, offset, chunk, total):
    n = order.devices
    step = block.shape[0] // n
    pick = (iota((n, block.shape[0]), 1) == iota((n, block.shape[0]), 0) * step + row).astype(BF)
    rows = dot(pick, block).astype(BF)
    lanes = block.shape[1]
    place = (iota((lanes, total), 0) == iota((lanes, total), 1) % chunk + offset).astype(BF)
    wide = dot(rows, place)
    mine = iota((n, total), 1) // chunk == owners(order, me, (n, total))
    return jnp.sum(jnp.where(mine, wide, 0.0), axis=0, keepdims=True)


def fold_lanes(order, me, vector, offset, chunk, lanes):
    n, total = order.devices, vector.shape[1]
    mine = iota((n, total), 1) // chunk == owners(order, me, (n, total))
    wide = jnp.where(mine, vector, 0.0).astype(BF)
    place = (iota((total, lanes), 1) == iota((total, lanes), 0) % chunk + offset).astype(BF)
    return dot(wide, place)


def place_rows(rows, row, step):
    n = rows.shape[0]
    pick = (iota((n * step, n), 0) == iota((n * step, n), 1) * step + row).astype(BF)
    return dot(pick, rows.astype(BF))


def live_column(lens, first, rows):
    position = first + iota((rows, 1), 0)
    start, live = 0, jnp.zeros((rows, 1), jnp.bool_)
    for i in range(lens.shape[1]):
        length = lens[0, i]
        live = live | ((position >= start) & (position < start + length))
        start = start + (length + BLOCK - 1) // BLOCK * BLOCK
    return live


def tile_bias(lens, tile, levels):
    position = tile * TILE + iota((1, TILE), 1)
    low, high, start = position, position + 1, 0
    for i in range(lens.shape[1]):
        length = lens[0, i]
        inside = (position >= start) & (position < start + length)
        low = jnp.where(inside, start, low)
        high = jnp.where(inside, start + length, high)
        start = start + (length + BLOCK - 1) // BLOCK * BLOCK
    parts = []
    for v in levels:
        begin = (v.first(tile) - v.pad + iota((v.window, TILE), 0)) * v.factor
        reach = (position // v.width - 1) * v.width
        valid = (begin >= low) & (begin + v.factor <= high) & (begin >= reach) & (begin < reach + 3 * v.width)
        if v.level > 0:
            half = v.width // 2
            lower = (position // half - 1) * half
            valid = valid & ~((begin >= lower) & (begin < lower + 3 * half))
        parts.append(jnp.where(valid, v.level * LOG_TWO, NEGATIVE))
    return jnp.concatenate(parts, axis=0)


def window_of(ref, tile, levels, lanes):
    return jnp.concatenate([ref[pl.ds(v.row(tile), v.window), lanes] for v in levels], axis=0)


def two_heads(rows):
    dim = rows.shape[1] // 2
    first = iota(rows.shape, 1) < dim
    zero = jnp.zeros_like(rows)
    return jnp.concatenate([jnp.where(first, rows, zero), jnp.where(first, zero, rows)], axis=0)


def own_heads(both):
    dim = both.shape[0] // 2
    return jnp.concatenate([both[:dim, :TILE], both[dim:, TILE:]], axis=0).T


def normalize(values):
    centre = values - jnp.mean(values, axis=-1, keepdims=True)
    scale = lax.rsqrt(jnp.mean(centre * centre, axis=-1, keepdims=True) + 1e-05)
    return centre * scale, scale


def norm_back(grad, normed, scale, gain):
    scaled = grad * gain
    return scale * (
        scaled
        - jnp.mean(scaled, axis=-1, keepdims=True)
        - normed * jnp.mean(scaled * normed, axis=-1, keepdims=True)
    )


def attend_kernel(
    order, seq, first_group, me_ref, lens_ref, x_ref, w_ref, vec_ref, fine_ref, wide_ref, *refs
):
    if first_group:
        p_ref, ctx_ref, q_ref, kx_ref, vx_ref, in_ref, w_scr = refs
    else:
        p_ref, ctx_ref, q_ref, kx_ref, vx_ref, w_scr = refs
    levels, total, _ = geometry(seq)
    near, far_base, *_ = pooling_shape(seq)
    tile = pl.program_id(0)
    lanes = q_ref.shape[1]
    me = me_ref[0]

    @pl.when(tile == 0)
    def _():
        unpack_rows(order, me, w_ref, slice(0, 3 * lanes), w_scr, w_ref.shape[0] // order.devices)
        if first_group:
            if order.stepped:
                chunk = x_ref.shape[1] // order.devices
                block = w_ref[:, 3 * lanes :]
                gain = spread_lanes(order, me, block, 0, 0, chunk, x_ref.shape[1])
                shift = spread_lanes(order, me, block, 0, chunk, chunk, x_ref.shape[1])
            else:
                gain, shift = vec_ref[0:1, :], vec_ref[1:2, :]
        kx_ref[...] = jnp.zeros_like(kx_ref)
        vx_ref[...] = jnp.zeros_like(vx_ref)
        step = 256
        for r in range(0, seq, step):
            if first_group:
                hat, _ = normalize(x_ref[r : r + step, :].astype(F32))
                first_in = (hat * gain + shift).astype(BF)
                in_ref[r : r + step, :] = first_in
            else:
                first_in = x_ref[r : r + step, :]
            joint = dot(first_in, w_scr[...]).astype(BF)
            q_ref[r : r + step, :] = joint[:, :lanes] * jnp.asarray(0.125, BF)
            pad = levels[0].pad
            kx_ref[pad + r : pad + r + step, :] = joint[:, lanes : 2 * lanes]
            vx_ref[pad + r : pad + r + step, :] = joint[:, 2 * lanes :]
        pad = levels[0].pad
        for ref in (kx_ref, vx_ref):
            for t in range(seq // TILE):
                rows = ref[pad + t * TILE : pad + (t + 1) * TILE, :]
                pooled = dot(fine_ref[...], rows).astype(BF)
                at = 0
                for v in near:
                    n = TILE // v.factor
                    ref[v.base + v.pad + t * n : v.base + v.pad + (t + 1) * n, :] = pooled[at : at + n]
                    at += n
            ref[far_base:total, :] = dot(wide_ref[...], ref[pad : pad + seq, :]).astype(BF)

    bias = tile_bias(lens_ref, tile, levels)
    bias = jnp.concatenate([bias, bias], axis=1)
    rows = pl.ds(pl.multiple_of(tile * TILE, TILE), TILE)
    for pair in range(lanes // TILE):
        cols = slice(pair * TILE, (pair + 1) * TILE)
        keys = window_of(kx_ref, tile, levels, cols)
        vals = window_of(vx_ref, tile, levels, cols)
        query = two_heads(q_ref[rows, cols])
        score = dot(keys, query, (1, 1)) + bias
        peak = jnp.max(score, axis=0, keepdims=True)
        weight = jnp.exp(score - peak)
        share = 1.0 / jnp.sum(weight, axis=0, keepdims=True)
        prob = (weight * share).astype(BF)
        p_ref[0, pair] = prob
        ctx_ref[:, cols] = own_heads(dot(vals, prob, (0, 0))).astype(BF)


def ffn_kernel(
    order,
    me_ref,
    lens_ref,
    x_ref,
    cot_ref,
    ctx0_ref,
    ctx1_ref,
    e_ref,
    r_ref,
    vec_ref,
    ebias_ref,
    mixed_ref,
    act_ref,
    eg_ref,
    in_ref,
    branch_ref,
    hg_ref,
    cg_ref,
    sums_ref,
    esum_ref,
    we_scr,
    wo_scr,
    wr_scr,
    vec_scr,
    eb_scr,
):
    tile = pl.program_id(0)
    me = me_ref[0]
    rows, d = x_ref.shape
    ff = we_scr.shape[1]
    half = ctx0_ref.shape[1]

    @pl.when(tile == 0)
    def _():
        chunk = d // order.devices
        unpack_rows(order, me, e_ref, slice(0, ff), we_scr, chunk)
        unpack_rows(order, me, e_ref, slice(ff, ff + d), wo_scr, chunk)
        unpack_rows(order, me, r_ref, slice(0, d), wr_scr, ff // order.devices)
        if order.stepped:
            block = e_ref[:, ff + d :]
            for k in range(3):
                vec_scr[k : k + 1, :] = spread_lanes(order, me, block, 0, k * chunk, chunk, d)
            eb_scr[...] = spread_lanes(order, me, block, 1, 0, ff // order.devices, ff)
        else:
            vec_scr[0:3, :] = vec_ref[2:5, :]
            eb_scr[...] = ebias_ref[...]
        sums_ref[...] = jnp.zeros_like(sums_ref)
        esum_ref[...] = jnp.zeros_like(esum_ref)

    gain, shift, rbias = vec_scr[0:1, :], vec_scr[1:2, :], vec_scr[2:3, :]
    live = live_column(lens_ref, tile * rows, rows).astype(F32)
    out = dot(ctx0_ref[...], wo_scr[:half, :]) + dot(ctx1_ref[...], wo_scr[half:, :])
    hidden = x_ref[...].astype(F32) + live * out
    hat, scale = normalize(hidden)
    second_in = (hat * gain + shift).astype(BF)
    in_ref[...] = second_in
    expanded = dot(second_in, we_scr[...]) + eb_scr[...]
    phi = 0.5 * (1.0 + lax.erf(expanded * ROOT_HALF))
    activated = (expanded * phi).astype(BF)
    act_ref[...] = activated
    slope = phi + expanded * (jnp.exp(-0.5 * expanded * expanded) * DENSITY)
    mixed_ref[...] = (hidden + live * (dot(activated, wr_scr[...]) + rbias)).astype(BF)
    cot = cot_ref[...].astype(F32)
    out_grad = (cot * live).astype(BF)
    expanded_grad = (dot(out_grad, wr_scr[...], (1, 1)) * slope).astype(BF)
    eg_ref[...] = expanded_grad
    second_grad = dot(expanded_grad, we_scr[...], (1, 1))
    sums_ref[0:1, :] += jnp.sum(second_grad * hat, axis=0, keepdims=True)
    sums_ref[1:2, :] += jnp.sum(second_grad, axis=0, keepdims=True)
    sums_ref[2:3, :] += jnp.sum(out_grad.astype(F32), axis=0, keepdims=True)
    esum_ref[...] += jnp.sum(expanded_grad.astype(F32), axis=0, keepdims=True)
    hidden_grad = cot + norm_back(second_grad, hat, scale, gain)
    hg_ref[...] = hidden_grad
    branch = (hidden_grad * live).astype(BF)
    branch_ref[...] = branch
    cg_ref[...] = dot(branch, wo_scr[...], (1, 1)).astype(BF)


def reduce_grad_kernel(order, me_ref, lens_ref, act_ref, cot_ref, out_ref, og_scr):
    step = pl.program_id(0)
    seq, d = cot_ref.shape
    cols = act_ref.shape[1]

    @pl.when(step == 0)
    def _():
        live = live_column(lens_ref, 0, seq).astype(F32)
        og_scr[...] = (cot_ref[...].astype(F32) * live).astype(BF)

    grad = dot(act_ref[...], og_scr[...], (0, 0)).astype(BF)
    chunk = out_ref.shape[0] // order.devices
    for k in range(cols // chunk):
        device = step * (cols // chunk) + k
        at = device
        if order.stepped:
            other, at = me_ref[0] ^ device, 0
            for b, bit in enumerate(order.bits):
                at = at + ((other // bit) & 1) * (1 << b)
        out_ref[pl.ds(pl.multiple_of(at * chunk, chunk), chunk), :] = grad[k * chunk : (k + 1) * chunk]


def expand_grad_kernel(
    order,
    me_ref,
    in_ref,
    eg_ref,
    ctx0_ref,
    ctx1_ref,
    branch_ref,
    sums_ref,
    esum_ref,
    e_ref,
    o_ref,
    scr_e,
    in_scr,
):
    step = pl.program_id(0)
    d = in_ref.shape[1]
    me = me_ref[0]
    chunk = d // order.devices

    @pl.when(step == 0)
    def _():
        in_scr[...] = in_ref[...].T
        both = jnp.concatenate([ctx0_ref[...], ctx1_ref[...]], axis=1)
        out = dot(both, branch_ref[...], (0, 0)).astype(BF)
        pack_rows(order, me, out, o_ref, slice(0, d), chunk, scr_e)
        if order.stepped:
            lanes = o_ref.shape[1] - d
            rows = jnp.zeros((order.devices, lanes), F32)
            for k in range(3):
                rows += fold_lanes(order, me, sums_ref[k : k + 1, :], k * chunk, chunk, lanes)
            ff = esum_ref.shape[1]
            more = fold_lanes(order, me, esum_ref[...], 0, ff // order.devices, lanes)
            o_ref[:, d:] = (place_rows(rows, 0, chunk) + place_rows(more, 1, chunk)).astype(BF)

    grad = dot(in_scr[...], eg_ref[...]).astype(BF)
    pack_rows(order, me, grad, e_ref, slice(None), chunk, scr_e)


def attend_back_kernel(
    order,
    seq,
    last,
    me_ref,
    p_ref,
    q_ref,
    cg_ref,
    kx_ref,
    vx_ref,
    in_ref,
    w_ref,
    spread_ref,
    *refs,
):
    if last:
        x_ref, fig0_ref, hg_ref, w0_ref, vec_ref, j_ref, tg_ref, sums_ref = refs[:8]
        dk_scr, dv_scr, dj_scr, w_scr, j_scr = refs[8:]
    else:
        j_ref, fig_ref = refs[:2]
        dk_scr, dv_scr, dj_scr, w_scr, j_scr = refs[2:]
    levels, total, _ = geometry(seq)
    near, far_base, *_ = pooling_shape(seq)
    tile = pl.program_id(0)
    lanes = q_ref.shape[1]
    me = me_ref[0]

    @pl.when(tile == 0)
    def _():
        dk_scr[...] = jnp.zeros_like(dk_scr)
        dv_scr[...] = jnp.zeros_like(dv_scr)
        unpack_rows(order, me, w_ref, slice(0, 3 * lanes), w_scr, w_ref.shape[0] // order.devices)

    rows = pl.ds(pl.multiple_of(tile * TILE, TILE), TILE)
    for pair in range(lanes // TILE):
        cols = slice(pair * TILE, (pair + 1) * TILE)
        keys = window_of(kx_ref, tile, levels, cols)
        vals = window_of(vx_ref, tile, levels, cols)
        query = two_heads(q_ref[:, cols])
        grad = two_heads(cg_ref[:, cols])
        prob = p_ref[0, pair]
        wide = prob.astype(F32)
        prob_grad = dot(vals, grad, (1, 1))
        inner = jnp.sum(wide * prob_grad, axis=0, keepdims=True)
        score_grad = (wide * (prob_grad - inner)).astype(BF)
        key_grad = dot(score_grad, query)
        val_grad = dot(prob, grad)
        dj_scr[rows, cols] = (own_heads(dot(keys, score_grad, (0, 0))) * 0.125).astype(BF)
        at = 0
        for v in levels:
            span = pl.ds(v.row(tile), v.window)
            dk_scr[span, cols] += key_grad[at : at + v.window]
            dv_scr[span, cols] += val_grad[at : at + v.window]
            at += v.window

    @pl.when(tile == pl.num_programs(0) - 1)
    def _():
        pad = levels[0].pad
        for ref, at in ((dk_scr, lanes), (dv_scr, 2 * lanes)):
            far = ref[far_base:total, :].astype(BF)
            for t in range(seq // TILE):
                parts = []
                for v in near:
                    n = TILE // v.factor
                    base = v.base + v.pad + t * n
                    parts.append(ref[base : base + n, :].astype(BF))
                parts.append(far)
                spread = dot(spread_ref[t * TILE : (t + 1) * TILE, :], jnp.concatenate(parts, axis=0))
                whole = ref[pad + t * TILE : pad + (t + 1) * TILE, :] + spread
                dj_scr[t * TILE : (t + 1) * TILE, at : at + lanes] = whole.astype(BF)
        joint = dot(in_ref[...], dj_scr[...], (0, 0)).astype(BF)
        chunk = joint.shape[0] // order.devices
        pack_rows(order, me, joint, j_ref, slice(0, 3 * lanes), chunk, j_scr)
        step = 256
        d = in_ref.shape[1]
        if last:
            if order.stepped:
                gain = spread_lanes(order, me, w0_ref[:, 3 * lanes :], 0, 0, chunk, d)
            else:
                gain = vec_ref[0:1, :]
            gains = jnp.zeros((1, d), F32)
            shifts = jnp.zeros((1, d), F32)
        for r in range(0, seq, step):
            fig = dot(dj_scr[r : r + step, :], w_scr[...], (1, 1))
            if not last:
                fig_ref[r : r + step, :] = fig
                continue
            fig = fig + fig0_ref[r : r + step, :]
            hat, scale = normalize(x_ref[r : r + step, :].astype(F32))
            gains += jnp.sum(fig * hat, axis=0, keepdims=True)
            shifts += jnp.sum(fig, axis=0, keepdims=True)
            grad = hg_ref[r : r + step, :] + norm_back(fig, hat, scale, gain)
            tg_ref[r : r + step, :] = grad.astype(BF)
        if last:
            sums_ref[0:1, :] = gains
            sums_ref[1:2, :] = shifts
            if order.stepped:
                extra = j_ref.shape[1] - 3 * lanes
                folded = fold_lanes(order, me, gains, 0, chunk, extra)
                folded += fold_lanes(order, me, shifts, chunk, chunk, extra)
                j_ref[:, 3 * lanes :] = place_rows(folded, 0, chunk).astype(BF)


def pooling_shape(seq):
    levels, total, _ = geometry(seq)
    near = [v for v in levels[1:] if v.width <= TILE]
    far = [v for v in levels[1:] if v.width > TILE]
    return near, far[0].base, total


def whole(shape):
    return pl.BlockSpec(shape, lambda i: (0,) * len(shape))


def smem():
    return pl.BlockSpec(memory_space=pltpu.SMEM)


def params(mib=56):
    return pltpu.CompilerParams(dimension_semantics=("arbitrary",), vmem_limit_bytes=mib * MIB)


def shape_of(shape, dtype):
    return jax.ShapeDtypeStruct(shape, dtype)


def attend(order, me, lens, x, w, vec, first_group):
    seq, d = x.shape
    lanes = d // GROUPS
    levels, total, window = geometry(seq)
    _, _, fine, wide, _ = pooling(seq)
    tiles = seq // TILE
    pairs = lanes // TILE
    outs = [
        (shape_of((tiles, pairs, window, 2 * TILE), BF), pl.BlockSpec((1, pairs, window, 2 * TILE), lambda i: (i, 0, 0, 0))),
        (shape_of((seq, lanes), BF), pl.BlockSpec((TILE, lanes), lambda i: (i, 0))),
        (shape_of((seq, lanes), BF), whole((seq, lanes))),
        (shape_of((total, lanes), BF), whole((total, lanes))),
        (shape_of((total, lanes), BF), whole((total, lanes))),
    ]
    if first_group:
        outs.append((shape_of((seq, d), BF), whole((seq, d))))
    return pl.pallas_call(
        functools.partial(attend_kernel, order, seq, first_group),
        grid=(tiles,),
        in_specs=[smem(), smem(), whole(x.shape), whole(w.shape), whole(vec.shape), whole(fine.shape), whole(wide.shape)],
        out_specs=[s for _, s in outs],
        out_shape=[o for o, _ in outs],
        scratch_shapes=[pltpu.VMEM((d, 3 * lanes), BF)],
        compiler_params=params(),
        cost_estimate=pl.CostEstimate(flops=4 * 10**9, bytes_accessed=10 * 10**6, transcendentals=2 * 10**6),
        name="attend",
    )(me, lens, x, w, vec, jnp.asarray(fine, BF), jnp.asarray(wide, BF))


def feed_forward(order, me, lens, x, cot, ctx0, ctx1, e, r, vec, ebias):
    seq, d = x.shape
    ff = r.shape[0]
    rows = 256

    def tiled(width):
        return pl.BlockSpec((rows, width), lambda i: (i, 0))

    outs = [
        (shape_of((seq, d), BF), tiled(d)),
        (shape_of((seq, ff), BF), tiled(ff)),
        (shape_of((seq, ff), BF), tiled(ff)),
        (shape_of((seq, d), BF), tiled(d)),
        (shape_of((seq, d), BF), tiled(d)),
        (shape_of((seq, d), F32), tiled(d)),
        (shape_of((seq, d), BF), tiled(d)),
        (shape_of((8, d), F32), whole((8, d))),
        (shape_of((1, ff), F32), whole((1, ff))),
    ]
    return pl.pallas_call(
        functools.partial(ffn_kernel, order),
        grid=(seq // rows,),
        in_specs=[
            smem(),
            smem(),
            tiled(d),
            tiled(d),
            tiled(ctx0.shape[1]),
            tiled(ctx1.shape[1]),
            whole(e.shape),
            whole(r.shape),
            whole(vec.shape),
            whole(ebias.shape),
        ],
        out_specs=[s for _, s in outs],
        out_shape=[o for o, _ in outs],
        scratch_shapes=[
            pltpu.VMEM((d, ff), BF),
            pltpu.VMEM((d, d), BF),
            pltpu.VMEM((ff, d), BF),
            pltpu.VMEM((8, d), F32),
            pltpu.VMEM((1, ff), F32),
        ],
        compiler_params=params(),
        cost_estimate=pl.CostEstimate(flops=10 * 10**9, bytes_accessed=20 * 10**6, transcendentals=4 * 10**6),
        name="ffn",
    )(me, lens, x, cot, ctx0, ctx1, e, r, vec, ebias)


def reduce_grads(order, me, lens, act, cot):
    seq, d = cot.shape
    ff = act.shape[1]
    cols = 256
    return pl.pallas_call(
        functools.partial(reduce_grad_kernel, order),
        grid=(ff // cols,),
        in_specs=[smem(), smem(), pl.BlockSpec((seq, cols), lambda i: (0, i)), whole((seq, d))],
        out_specs=whole((ff, d)),
        out_shape=shape_of((ff, d), BF),
        scratch_shapes=[pltpu.VMEM((seq, d), BF)],
        compiler_params=params(),
        cost_estimate=pl.CostEstimate(flops=2 * 10**9, bytes_accessed=8 * 10**6, transcendentals=0),
        name="reduce_grad",
    )(me, lens, act, cot)


def expand_grads(order, me, second_in, eg, ctx0, ctx1, branch, sums, esum):
    seq, d = second_in.shape
    ff = eg.shape[1]
    cols = 512
    extra = 128 if order.stepped else 0
    return pl.pallas_call(
        functools.partial(expand_grad_kernel, order),
        grid=(ff // cols,),
        in_specs=[
            smem(),
            whole((seq, d)),
            pl.BlockSpec((seq, cols), lambda i: (0, i)),
            whole(ctx0.shape),
            whole(ctx1.shape),
            whole(branch.shape),
            whole(sums.shape),
            whole(esum.shape),
        ],
        out_specs=[pl.BlockSpec((d, cols), lambda i: (0, i)), whole((d, d + extra))],
        out_shape=[shape_of((d, ff), BF), shape_of((d, d + extra), BF)],
        scratch_shapes=[pltpu.VMEM((d, cols), BF), pltpu.VMEM((d, seq), BF)],
        compiler_params=params(),
        cost_estimate=pl.CostEstimate(flops=3 * 10**9, bytes_accessed=10 * 10**6, transcendentals=0),
        name="expand_grad",
    )(me, second_in, eg, ctx0, ctx1, branch, sums, esum)


def attend_back(order, me, group, prob, q, cg, kx, vx, first_in, w, tail=None):
    seq, d = first_in.shape
    lanes = d // GROUPS
    levels, total, window = geometry(seq)
    spread = pooling(seq)[4]
    tiles, pairs = prob.shape[:2]
    last = tail is not None
    extra = 128 if order.stepped and last else 0
    ins = [
        (me, smem()),
        (prob, pl.BlockSpec((1, pairs, window, 2 * TILE), lambda i: (i, 0, 0, 0))),
        (q, pl.BlockSpec((TILE, lanes), lambda i: (i, 0))),
        (cg, pl.BlockSpec((TILE, lanes), lambda i: (i, group))),
        (kx, whole(kx.shape)),
        (vx, whole(vx.shape)),
        (first_in, whole(first_in.shape)),
        (w, whole(w.shape)),
        (jnp.asarray(spread, BF), whole(spread.shape)),
    ]
    outs = [(shape_of((d, 3 * lanes + extra), BF), whole((d, 3 * lanes + extra)))]
    if last:
        ins += [(a, whole(a.shape)) for a in tail]
        outs.append((shape_of((seq, d), BF), whole((seq, d))))
        outs.append((shape_of((8, d), F32), whole((8, d))))
    else:
        outs.append((shape_of((seq, d), F32), whole((seq, d))))
    return pl.pallas_call(
        functools.partial(attend_back_kernel, order, seq, last),
        grid=(tiles,),
        in_specs=[s for _, s in ins],
        out_specs=[s for _, s in outs],
        out_shape=[o for o, _ in outs],
        scratch_shapes=[
            pltpu.VMEM((total, lanes), F32),
            pltpu.VMEM((total, lanes), F32),
            pltpu.VMEM((seq, 3 * lanes), BF),
            pltpu.VMEM((d, 3 * lanes), BF),
            pltpu.VMEM((d, 3 * lanes), BF),
        ],
        compiler_params=params(),
        cost_estimate=pl.CostEstimate(flops=6 * 10**9, bytes_accessed=15 * 10**6, transcendentals=0),
        name="attend_back",
    )(*[a for a, _ in ins])


def swap(order, value, bit):
    return lax.ppermute(value, AXES, [(i, i ^ bit) for i in range(order.devices)])


def gather_rows(order, value):
    if not order.stepped:
        return lax.all_gather(value, AXES, axis=0, tiled=True)
    for bit in order.bits:
        value = jnp.concatenate([value, swap(order, value, bit)], axis=0)
    return value


def scatter_sum(order, value):
    if not order.stepped:
        return lax.psum_scatter(value.astype(F32), AXES, scatter_dimension=0, tiled=True)
    for bit in reversed(order.bits):
        half = value.shape[0] // 2
        other = swap(order, value[half:], bit)
        value = value[:half].astype(F32) + other.astype(F32)
        if bit != order.bits[0]:
            value = value.astype(BF)
    return value


def local(order, me, gather, scatter, tokens, cotangent, lens, joint, output_w, expand, reduce_w,
          attn_gain, attn_shift, ffn_gain, ffn_shift, expand_bias, reduce_bias):
    seq, d = tokens.shape
    lanes = d // GROUPS
    rows = joint.shape[0]
    ff = expand.shape[1]

    def group_columns(g):
        return [joint[:, k * d + g * lanes : k * d + (g + 1) * lanes] for k in range(3)]

    def as_rows(vectors):
        flat = jnp.concatenate(vectors)
        return jnp.pad(flat, (0, 128 - flat.shape[0]))[None]

    if order.stepped:
        blank = jnp.zeros((rows - 1, 128), BF)
        vec_a = jnp.concatenate([as_rows([attn_gain, attn_shift]), blank], axis=0)
        vec_e = jnp.concatenate(
            [as_rows([ffn_gain, ffn_shift, reduce_bias]), as_rows([expand_bias]), blank[1:]], axis=0
        )
        w0 = gather(jnp.concatenate(group_columns(0) + [vec_a], axis=1))
        w1 = gather(jnp.concatenate(group_columns(1), axis=1))
        e = gather(jnp.concatenate([expand, output_w, vec_e], axis=1))
        r = gather(reduce_w)
        vec = jnp.zeros((8, d), F32)
        ebias = jnp.zeros((1, ff), F32)
    else:
        w0 = gather(jnp.concatenate(group_columns(0), axis=1))
        w1 = gather(jnp.concatenate(group_columns(1), axis=1))
        e = gather(jnp.concatenate([expand, output_w], axis=1))
        r = gather(reduce_w)
        small = [gather(v) for v in (attn_gain, attn_shift, ffn_gain, ffn_shift, reduce_bias)]
        vec = jnp.pad(jnp.stack(small), ((0, 3), (0, 0))).astype(F32)
        ebias = gather(expand_bias)[None].astype(F32)

    p0, ctx0, q0, kx0, vx0, first_in = attend(order, me, lens, tokens, w0, vec, True)
    p1, ctx1, q1, kx1, vx1 = attend(order, me, lens, first_in, w1, vec, False)
    mixed, act, eg, second_in, branch, hg, cg, sums, esum = feed_forward(
        order, me, lens, tokens, cotangent, ctx0, ctx1, e, r, vec, ebias
    )
    rg = reduce_grads(order, me, lens, act, cotangent)
    eg_out, og_out = expand_grads(order, me, second_in, eg, ctx0, ctx1, branch, sums, esum)
    j0, fig0 = attend_back(order, me, 0, p0, q0, cg, kx0, vx0, first_in, w0)
    j1, token_grad, tail_sums = attend_back(
        order, me, 1, p1, q1, cg, kx1, vx1, first_in, w1, (tokens, fig0, hg, w0, vec)
    )
    reduce_grad = scatter(rg)
    expand_out = scatter(jnp.concatenate([eg_out, og_out], axis=1))
    j0 = scatter(j0)
    j1 = scatter(j1)
    parts = []
    for k in range(3):
        parts += [j0[:, k * lanes : (k + 1) * lanes], j1[:, k * lanes : (k + 1) * lanes]]
    joint_grad = jnp.concatenate(parts, axis=1)
    expand_grad = expand_out[:, :ff]
    output_grad = expand_out[:, ff : ff + d]
    if order.stepped:
        tail = j1[0, 3 * lanes :]
        body = expand_out[0, ff + d :]
        small = [tail[:rows], tail[rows : 2 * rows]]
        small += [body[k * rows : (k + 1) * rows] for k in range(3)]
        small.insert(4, expand_out[1, ff + d : ff + d + ff // order.devices])
    else:
        small = [scatter(tail_sums[0]), scatter(tail_sums[1])]
        small += [scatter(sums[0]), scatter(sums[1]), scatter(esum[0]), scatter(sums[2])]
    return (mixed, token_grad, joint_grad, output_grad, expand_grad, reduce_grad, *small)


def shards(order, *args):
    sub = lax.axis_size("sub")
    me = (lax.axis_index("dp") * sub + lax.axis_index("sub")).astype(jnp.int32).reshape(1)
    return local(
        order,
        me,
        functools.partial(gather_rows, order),
        functools.partial(scatter_sum, order),
        *args,
    )


def solution(mesh):
    order = Order(math.prod(mesh.shape[a] for a in AXES))
    wide = P(AXES, None)
    flat = P(AXES)
    return jax.shard_map(
        functools.partial(shards, order),
        mesh=mesh,
        in_specs=(wide,) * 7 + (flat,) * 6,
        out_specs=(wide,) * 6 + (flat,) * 6,
        check_vma=False,
    )
```

time: 1400 us -> 253 us (0.18)
  local copies, waits for them, and re-layouts: 561 us -> 28.6 us
  waiting for transfers between devices: 302 us -> 67.3 us
  matrix products: 212 us -> 0 us
  other arithmetic: 169 us -> 7.65 us
  blocking collectives: 125 us -> 0 us
  Pallas kernels: 0 us -> 101 us
  starting transfers between devices: 0.28 us -> 47.2 us
  between operations: 17.5 us -> 1.15 us
    reduce_scatter x4 -> x0, waiting for transfers between devices: 300 us -> none  [the longest x1 144 us: return_grads(): lax.psum_scatter(reduce_w, ('dp', 'sub'), scatter_dimension=0, tiled=True)]
    dot_general x54 -> x0, matrix products: 212 us -> none  [the longest x7 29.7 us: attend_back(): jnp.einsum('bhwj,bwhd->bjhd', weight.astype(jnp.bfloat16), grad_block, pr...]
    reshape x130 -> x0, local copies, waits for them, and re-layouts: 200 us -> none  [the longest x108 105 us: to_rows(): return reduced.transpose(0, 2, 1).reshape(-1, reduced.shape[1])]
    pallas_call x0 -> x7, Pallas kernels: none -> 101 us  [the longest x2 35.6 us: attend_back(): pl.pallas_call(functools.partial(attend_back_kernel, order, seq, last), g...]
    unnamed x2 -> x0, blocking collectives: 80.5 us -> none
    ppermute x0 -> x40, waiting for transfers between devices: none -> 67.3 us  [swap(): lax.ppermute(value, AXES, [(i, i ^ bit) for i in range(order.devices)])]
    div x24 -> x0, local copies, waits for them, and re-layouts: 66.6 us -> none  [spread_out(): return jnp.repeat(grad, factor, axis=0) / factor]
    reduce_sum x26 -> x0, other arithmetic: 63.7 us -> none  [the longest x12 37.7 us: coarse(): return jnp.mean(grouped, axis=1).astype(jnp.bfloat16)]
  transfers between devices with their start and end apart: 7 -> 40, of which waited for: 3 -> 14; matrix products, arithmetic and copies ran while one was open for 51% -> 11% of each run, Pallas kernels for 0% -> 26%
where the time goes in v1:
time: 253 us; the launch traced here: 252 us
  Pallas kernels  101 us (40%)
  waiting for transfers between devices  67.3 us (27%)
  starting transfers between devices  47.2 us (19%)
  local copies, waits for them, and re-layouts  28.6 us (11%)
  other arithmetic  7.65 us (3%)
    ppermute x40, waiting for transfers between devices, swap(): lax.ppermute(value, AXES, [(i, i ^ bit) for i in range(order.devices)])  67.3 us
    ppermute x40, starting transfers between devices, swap(): lax.ppermute(value, AXES, [(i, i ^ bit) for i in range(order.devices)])  47.2 us
    pallas_call x2, Pallas kernels, attend_back(): pl.pallas_call(functools.partial(attend_back_kernel, order, seq, last), g...  35.6 us
    pallas_call x2, Pallas kernels, attend(): pl.pallas_call(functools.partial(attend_kernel, order, seq, first_group),...  28.7 us
    pallas_call x1, Pallas kernels, feed_forward(): pl.pallas_call(functools.partial(ffn_kernel, order), grid=(seq // rows,),...  18.8 us
    unnamed x51, local copies, waits for them, and re-layouts  14.3 us
    pallas_call x1, Pallas kernels, reduce_grads(): pl.pallas_call(functools.partial(reduce_grad_kernel, order), grid=(ff //...  9.44 us
    pallas_call x1, Pallas kernels, expand_grads(): pl.pallas_call(functools.partial(expand_grad_kernel, order), grid=(ff //...  7.97 us
  transfers between devices with their start and end apart: 40, of which 14 were waited for; matrix products, arithmetic and copies ran while one was open for 11% of the time, Pallas kernels for 26%

profile of v1, /device:TPU:0, one launch (start us, length us, event | category | flops | bytes accessed | tf_op | source)
XLA Modules:
  0.0 252.5 jit_solution(514286929568143567)
XLA Ops:
  0.7 4.1 %collective-permute-start.15 = (bf16[64,512]{1,0:T(8,128)(2,1)}, bf16[64,512]{1,0:T(8,128)(2,1)S(1)}, u32[]{:S(2)}, u32[]{:S(2)}) collective-permute-start(bf16[64,512]{1,0:T(8,128)(2,1)} %param.25), channel_id=1, source_target_pairs={{0,16},{1,17},{2,18},{3,19},{4,20},{5,21},{6,22},{7,23},{8,24},{9,... | collective-permute-start | bytes 196616 | tf_op jit(solution)/shard_map/ppermute | solution.py:722
  7.6 2.9 %collective-permute-start = (bf16[16,896]{1,0:T(8,128)(2,1)S(1)}, bf16[16,896]{1,0:T(8,128)(2,1)S(1)}, u32[]{:S(2)}, u32[]{:S(2)}) collective-permute-start(bf16[16,896]{1,0:T(8,128)(2,1)S(1)} %get-tuple-element.112), channel_id=1, source_target_pairs={{0,16},{1,17},{2,18},{3,19},{4,20},{5,21},{6,22},{7,23},{8,24},{9,... | collective-permute-start | bytes 86024 | tf_op jit(solution)/shard_map/ppermute | solution.py:722
  33.0 8.2 %collective-permute-done.12 = bf16[64,2688]{1,0:T(8,128)(2,1)S(1)} collective-permute-done((bf16[64,2688]{1,0:T(8,128)(2,1)S(1)}, bf16[64,2688]{1,0:T(8,128)(2,1)S(1)}, u32[]{:S(2)}, u32[]{:S(2)}) %collective-permute-start.12) | collective-permute-done | bytes 344096 | tf_op jit(solution)/shard_map/ppermute | solution.py:722
  46.7 13.0 %collective-permute-done.13 = bf16[128,2688]{1,0:T(8,128)(2,1)S(1)} collective-permute-done((bf16[128,2688]{1,0:T(8,128)(2,1)S(1)}, bf16[128,2688]{1,0:T(8,128)(2,1)S(1)}, u32[]{:S(2)}, u32[]{:S(2)}) %collective-permute-start.13) | collective-permute-done | bytes 688160 | tf_op jit(solution)/shard_map/ppermute | solution.py:722
  61.4 4.9 %collective-permute-done.18 = bf16[512,512]{1,0:T(8,128)(2,1)S(1)} collective-permute-done((bf16[512,512]{1,0:T(8,128)(2,1)S(1)}, bf16[512,512]{1,0:T(8,128)(2,1)S(1)}, u32[]{:S(2)}, u32[]{:S(2)}) %collective-permute-start.18) | collective-permute-done | bytes 524320 | tf_op jit(solution)/shard_map/ppermute | solution.py:722
  70.8 14.6 %attend.2 = (bf16[8,2,464,256]{3,2,1,0:T(8,128)(2,1)}, bf16[1024,256]{1,0:T(8,128)(2,1)}, bf16[1024,256]{1,0:T(8,128)(2,1)}, bf16[2192,256]{1,0:T(8,128)(2,1)}, ...) custom-call(s32[1]{0:T(128)} %bitcast.me_ref, s32[1,8]{1,0:T(1,128)} %lens_ref.7, bf16[1024,512]{1,0:T(8,128)(2,1)} %refs_0_.1, ...), custom_call_target="tpu_custom_call" | custom-call | flops 4000000000 | bytes 10000000 | tf_op jit(solution)/shard_map/attend/pallas_call | solution.py:570
  85.4 14.1 %attend.3 = (bf16[8,2,464,256]{3,2,1,0:T(8,128)(2,1)}, bf16[1024,256]{1,0:T(8,128)(2,1)}, bf16[1024,256]{1,0:T(8,128)(2,1)}, bf16[2192,256]{1,0:T(8,128)(2,1)}, bf16[2192,256]{1,0:T(8,128)(2,1)}) custom-call(s32[1]{0:T(128)} %bitcast.me_ref, s32[1,8]{1,0:T(1,128)} %lens_ref.7, bf16[1024,512]{1,0:T(8,128)(2,1)} %get-tuple-element.39.x_ref.in_ref, ...), custom_call_target="tpu_custom_call" | custom-call | flops 4000000000 | bytes 10000000 | tf_op jit(solution)/shard_map/attend/pallas_call | solution.py:570
  101.7 18.8 %ffn.1 = (bf16[1024,512]{1,0:T(8,128)(2,1)}, bf16[1024,2048]{1,0:T(8,128)(2,1)}, bf16[1024,2048]{1,0:T(8,128)(2,1)}, bf16[1024,512]{1,0:T(8,128)(2,1)}, bf16[102...) custom-call(s32[1]{0:T(128)} %bitcast.me_ref, ...), custom_call_target="tpu_custom_call" | custom-call | flops 10000000000 | bytes 20000000 | tf_op jit(solution)/shard_map/ffn/pallas_call | solution.py:602
  120.6 16.6 %attend_back.2 = (bf16[512,768]{1,0:T(8,128)(2,1)}, f32[1024,512]{1,0:T(8,128)}) custom-call(s32[1]{0:T(128)} %bitcast.me_ref, bf16[8,2,464,256]{3,2,1,0:T(8,128)(2,1)} %get-tuple-element.47.p_ref, bf16[1024,256]{1,0:T(8,128)(2,1)} %get-tuple-element.48.q_ref, bf16[1024,512]{1,0:T(8,128)(2,1)} %get-tuple-element.44.cg_ref, ...), custom_call_target="tpu_custom_call" | custom-call | flops 6000000000 | bytes 15000000 | tf_op jit(solution)/shard_map/attend_back/pallas_call | solution.py:702
  138.8 19.1 %attend_back.3 = (bf16[512,896]{1,0:T(8,128)(2,1)}, bf16[1024,512]{1,0:T(8,128)(2,1)}, f32[8,512]{1,0:T(8,128)}) custom-call(s32[1]{0:T(128)} %bitcast.me_ref, bf16[8,2,464,256]{3,2,1,0:T(8,128)(2,1)} %get-tuple-element.42.p_ref, bf16[1024,256]{1,0:T(8,128)(2,1)} %get-tuple-element.43.q_ref, bf16[1024,512]{1,0:T(8,128)(2,1)} %get-tuple-element.44.cg_ref, ...), custom_call_target="tpu_custom_call" | custom-call | flops 6000000000 | bytes 15000000 | tf_op jit(solution)/shard_map/attend_back/pallas_call | solution.py:702
  159.0 8.0 %expand_grad.1 = (bf16[512,2048]{1,0:T(8,128)(2,1)}, bf16[512,640]{1,0:T(8,128)(2,1)}) custom-call(s32[1]{0:T(128)} %bitcast.me_ref, bf16[1024,512]{1,0:T(8,128)(2,1)} %get-tuple-element.56.in_ref, bf16[1024,2048]{1,0:T(8,128)(2,1)} %get-tuple-element.57.eg_ref, bf16[1024,256]{1,0:T(8,128)(2,1)} %get-tuple-element.38.ctx0_ref, ...), custom_call_target="tpu_custom_call" | custom-call | flops 3000000000 | bytes 10000000 | tf_op jit(solution)/shard_map/expand_grad/pallas_call | solution.py:654
  170.6 9.4 %reduce_grad.1 = bf16[2048,512]{1,0:T(8,128)(2,1)} custom-call(s32[1]{0:T(128)} %bitcast.me_ref, s32[1,8]{1,0:T(1,128)} %lens_ref.7, bf16[1024,2048]{1,0:T(8,128)(2,1)} %get-tuple-element.63.act_ref, bf16[1024,512]{1,0:T(8,128)(2,1)} %cot_ref.3), custom_call_target="tpu_custom_call" | custom-call | flops 2000000000 | bytes 8000000 | tf_op jit(solution)/shard_map/reduce_grad/pallas_call | solution.py:636
  183.5 3.8 %collective-permute-done.22 = bf16[64,768]{1,0:T(8,128)(2,1)S(1)} collective-permute-done((bf16[64,768]{1,0:T(8,128)(2,1)S(1)}, bf16[64,768]{1,0:T(8,128)(2,1)S(1)}, u32[]{:S(2)}, u32[]{:S(2)}) %collective-permute-start.22) | collective-permute-done | bytes 98336 | tf_op jit(solution)/shard_map/ppermute | solution.py:722
  192.2 2.7 %collective-permute-start.24 = (bf16[16,768]{1,0:T(8,128)(2,1)S(1)}, bf16[16,768]{1,0:T(8,128)(2,1)S(1)}, u32[]{:S(2)}, u32[]{:S(2)}) collective-permute-start(bf16[16,768]{1,0:T(8,128)(2,1)S(1)} %slice.278), channel_id=1, source_target_pairs={{0,16},{1,17},{2,18},{3,19},{4,20},{5,21},{6,22},{7,23},{8,24},{9,... | collective-permute-start | bytes 73736 | tf_op jit(solution)/shard_map/ppermute | solution.py:722
  197.5 2.6 %collective-permute-done.28 = bf16[32,896]{1,0:T(8,128)(2,1)S(1)} collective-permute-done((bf16[32,896]{1,0:T(8,128)(2,1)S(1)}, bf16[32,896]{1,0:T(8,128)(2,1)S(1)}, u32[]{:S(2)}, u32[]{:S(2)}) %collective-permute-start.28) | collective-permute-done | bytes 57376 | tf_op jit(solution)/shard_map/ppermute | solution.py:722
  200.1 2.7 %collective-permute-start.29 = (bf16[16,896]{1,0:T(8,128)(2,1)S(1)}, bf16[16,896]{1,0:T(8,128)(2,1)S(1)}, u32[]{:S(2)}, u32[]{:S(2)}) collective-permute-start(bf16[16,896]{1,0:T(8,128)(2,1)S(1)} %slice.287), channel_id=1, source_target_pairs={{0,16},{1,17},{2,18},{3,19},{4,20},{5,21},{6,22},{7,23},{8,24},{9,... | collective-permute-start | bytes 86024 | tf_op jit(solution)/shard_map/ppermute | solution.py:722
  202.8 2.2 collective-permute-done.29
  208.0 12.3 %collective-permute-done.36 = bf16[512,512]{1,0:T(8,128)(2,1)S(1)} collective-permute-done((bf16[512,512]{1,0:T(8,128)(2,1)S(1)}, bf16[512,512]{1,0:T(8,128)(2,1)S(1)}, u32[]{:S(2)}, u32[]{:S(2)}) %collective-permute-start.36) | collective-permute-done | bytes 524320 | tf_op jit(solution)/shard_map/ppermute | solution.py:722
  221.7 8.5 %collective-permute-done.31 = bf16[128,2688]{1,0:T(8,128)(2,1)S(1)} collective-permute-done((bf16[128,2688]{1,0:T(8,128)(2,1)S(1)}, bf16[128,2688]{1,0:T(8,128)(2,1)S(1)}, u32[]{:S(2)}, u32[]{:S(2)}) %collective-permute-start.31) | collective-permute-done | bytes 688160 | tf_op jit(solution)/shard_map/ppermute | solution.py:722
  233.9 3.8 %collective-permute-done.32 = bf16[64,2688]{1,0:T(8,128)(2,1)S(1)} collective-permute-done((bf16[64,2688]{1,0:T(8,128)(2,1)S(1)}, bf16[64,2688]{1,0:T(8,128)(2,1)S(1)}, u32[]{:S(2)}, u32[]{:S(2)}) %collective-permute-start.32) | collective-permute-done | bytes 344096 | tf_op jit(solution)/shard_map/ppermute | solution.py:722
  239.7 2.6 %collective-permute-start.39 = (bf16[64,512]{1,0:T(8,128)(2,1)S(1)}, bf16[64,512]{1,0:T(8,128)(2,1)S(1)}, u32[]{:S(2)}, u32[]{:S(2)}) collective-permute-start(bf16[64,512]{1,0:T(8,128)(2,1)S(1)} %slice.314), channel_id=1, source_target_pairs={{0,16},{1,17},{2,18},{3,19},{4,20},{5,21},{6,22},{7,23},{8,24},{9,... | collective-permute-start | bytes 196616 | tf_op jit(solution)/shard_map/ppermute | solution.py:722
  242.3 2.2 collective-permute-done.33
  244.6 2.3 collective-permute-start.34
  247.6 2.5 collective-permute-done.34
  (191 shorter events, 69.5 us)
Async XLA Ops:
  0.7 17.0 %collective-permute-start.15 = (bf16[64,512]{1,0:T(8,128)(2,1)}, bf16[64,512]{1,0:T(8,128)(2,1)S(1)}, u32[]{:S(2)}, u32[]{:S(2)}) collective-permute-start(bf16[64,512]{1,0:T(8,128)(2,1)} %param.25), channel_id=1, source_target_pairs={{0,16},{1,17},{2,18},{3,19},{4,20},{5,21},{6,22},{7,23},{8,24},{9,... | collective-permute-start | bytes 196616 | tf_op jit(solution)/shard_map/ppermute | solution.py:722
  6.2 8.1 %collective-permute-start.5 = (bf16[16,768]{1,0:T(8,128)(2,1)S(1)}, bf16[16,768]{1,0:T(8,128)(2,1)S(1)}, u32[]{:S(2)}, u32[]{:S(2)}) collective-permute-start(bf16[16,768]{1,0:T(8,128)(2,1)S(1)} %get-tuple-element.117), channel_id=1, source_target_pairs={{0,16},{1,17},{2,18},{3,19},{4,20},{5,21},{6,22},{7,23},{8,24},{9,... | collective-permute-start | bytes 73736 | tf_op jit(solution)/shard_map/ppermute | solution.py:722
  7.6 9.3 %collective-permute-start = (bf16[16,896]{1,0:T(8,128)(2,1)S(1)}, bf16[16,896]{1,0:T(8,128)(2,1)S(1)}, u32[]{:S(2)}, u32[]{:S(2)}) collective-permute-start(bf16[16,896]{1,0:T(8,128)(2,1)S(1)} %get-tuple-element.112), channel_id=1, source_target_pairs={{0,16},{1,17},{2,18},{3,19},{4,20},{5,21},{6,22},{7,23},{8,24},{9,... | collective-permute-start | bytes 86024 | tf_op jit(solution)/shard_map/ppermute | solution.py:722
  12.8 11.2 %collective-permute-start.10 = (bf16[16,2688]{1,0:T(8,128)(2,1)S(1)}, bf16[16,2688]{1,0:T(8,128)(2,1)S(1)}, u32[]{:S(2)}, u32[]{:S(2)}) collective-permute-start(bf16[16,2688]{1,0:T(8,128)(2,1)S(1)} %get-tuple-element.89), channel_id=1, source_target_pairs={{0,16},{1,17},{2,18},{3,19},{4,20},{5,21},{6,22},{7,23},{8,24},{9,... | collective-permute-start | bytes 258056 | tf_op jit(solution)/shard_map/ppermute | solution.py:722
  18.5 9.6 %collective-permute-start.16 = (bf16[128,512]{1,0:T(8,128)(2,1)S(1)}, bf16[128,512]{1,0:T(8,128)(2,1)S(1)}, u32[]{:S(2)}, u32[]{:S(2)}) collective-permute-start(bf16[128,512]{1,0:T(8,128)(2,1)S(1)} %pad_maximum_fusion.7), channel_id=1, source_target_pairs={{0,8},{1,9},{2,10},{3,11},{4,12},{5,13},{6,14},{7,15},{8,0},{9,1},... | collective-permute-start | bytes 393224 | tf_op jit(solution)/shard_map/ppermute | solution.py:722
  25.9 16.5 %collective-permute-start.8 = (bf16[128,768]{1,0:T(8,128)(2,1)S(1)}, bf16[128,768]{1,0:T(8,128)(2,1)S(1)}, u32[]{:S(2)}, u32[]{:S(2)}) collective-permute-start(bf16[128,768]{1,0:T(8,128)(2,1)S(1)} %pad_maximum_fusion.5), channel_id=1, source_target_pairs={{0,2},{1,3},{2,0},{3,1},{4,6},{5,7},{6,4},{7,5},{8,10},{9,11},{10,... | collective-permute-start | bytes 589832 | tf_op jit(solution)/shard_map/ppermute | solution.py:722
  28.1 16.7 %collective-permute-start.17 = (bf16[256,512]{1,0:T(8,128)(2,1)S(1)}, bf16[256,512]{1,0:T(8,128)(2,1)S(1)}, u32[]{:S(2)}, u32[]{:S(2)}) collective-permute-start(bf16[256,512]{1,0:T(8,128)(2,1)S(1)} %pad_maximum_fusion.3), channel_id=1, source_target_pairs={{0,4},{1,5},{2,6},{3,7},{4,0},{5,1},{6,2},{7,3},{8,12},{9,13},{10,... | collective-permute-start | bytes 786440 | tf_op jit(solution)/shard_map/ppermute | solution.py:722
  30.4 12.7 %collective-permute-start.3 = (bf16[128,896]{1,0:T(8,128)(2,1)S(1)}, bf16[128,896]{1,0:T(8,128)(2,1)S(1)}, u32[]{:S(2)}, u32[]{:S(2)}) collective-permute-start(bf16[128,896]{1,0:T(8,128)(2,1)S(1)} %pad_maximum_fusion.4), channel_id=1, source_target_pairs={{0,2},{1,3},{2,0},{3,1},{4,6},{5,7},{6,4},{7,5},{8,10},{9,11},{10,... | collective-permute-start | bytes 688136 | tf_op jit(solution)/shard_map/ppermute | solution.py:722
  31.7 9.5 %collective-permute-start.12 = (bf16[64,2688]{1,0:T(8,128)(2,1)S(1)}, bf16[64,2688]{1,0:T(8,128)(2,1)S(1)}, u32[]{:S(2)}, u32[]{:S(2)}) collective-permute-start(bf16[64,2688]{1,0:T(8,128)(2,1)S(1)} %pad_maximum_fusion.2), channel_id=1, source_target_pairs={{0,4},{1,5},{2,6},{3,7},{4,0},{5,1},{6,2},{7,3},{8,12},{9,13},{10,... | collective-permute-start | bytes 1032200 | tf_op jit(solution)/shard_map/ppermute | solution.py:722
  41.2 18.4 %collective-permute-start.13 = (bf16[128,2688]{1,0:T(8,128)(2,1)S(1)}, bf16[128,2688]{1,0:T(8,128)(2,1)S(1)}, u32[]{:S(2)}, u32[]{:S(2)}) collective-permute-start(bf16[128,2688]{1,0:T(8,128)(2,1)S(1)} %pad_maximum_fusion), channel_id=1, source_target_pairs={{0,2},{1,3},{2,0},{3,1},{4,6},{5,7},{6,4},{7,5},{8,10},{9,11},{10,... | collective-permute-start | bytes 2064392 | tf_op jit(solution)/shard_map/ppermute | solution.py:722
  43.0 25.5 %collective-permute-start.9 = (bf16[256,768]{1,0:T(8,128)(2,1)}, bf16[256,768]{1,0:T(8,128)(2,1)S(1)}, u32[]{:S(2)}, u32[]{:S(2)}) collective-permute-start(bf16[256,768]{1,0:T(8,128)(2,1)} %get-tuple-element.74), channel_id=1, source_target_pairs={{0,1},{1,0},{2,3},{3,2},{4,5},{5,4},{6,7},{7,6},{8,9},{9,8},{10,11... | collective-permute-start | bytes 1179656 | tf_op jit(solution)/shard_map/ppermute | solution.py:722
  43.9 25.5 %collective-permute-start.4 = (bf16[256,896]{1,0:T(8,128)(2,1)}, bf16[256,896]{1,0:T(8,128)(2,1)S(1)}, u32[]{:S(2)}, u32[]{:S(2)}) collective-permute-start(bf16[256,896]{1,0:T(8,128)(2,1)} %get-tuple-element.72), channel_id=1, source_target_pairs={{0,1},{1,0},{2,3},{3,2},{4,5},{5,4},{6,7},{7,6},{8,9},{9,8},{10,11... | collective-permute-start | bytes 1376264 | tf_op jit(solution)/shard_map/ppermute | solution.py:722
  44.9 21.5 %collective-permute-start.18 = (bf16[512,512]{1,0:T(8,128)(2,1)S(1)}, bf16[512,512]{1,0:T(8,128)(2,1)S(1)}, u32[]{:S(2)}, u32[]{:S(2)}) collective-permute-start(bf16[512,512]{1,0:T(8,128)(2,1)S(1)} %pad_maximum_fusion.1), channel_id=1, source_target_pairs={{0,2},{1,3},{2,0},{3,1},{4,6},{5,7},{6,4},{7,5},{8,10},{9,11},{10,... | collective-permute-start | bytes 1572872 | tf_op jit(solution)/shard_map/ppermute | solution.py:722
  60.6 39.0 %collective-permute-start.14 = (bf16[256,2688]{1,0:T(8,128)(2,1)}, bf16[256,2688]{1,0:T(8,128)(2,1)S(1)}, u32[]{:S(2)}, u32[]{:S(2)}) collective-permute-start(bf16[256,2688]{1,0:T(8,128)(2,1)} %get-tuple-element.64), channel_id=1, source_target_pairs={{0,1},{1,0},{2,3},{3,2},{4,5},{5,4},{6,7},{7,6},{8,9},{9,8},{10,11... | collective-permute-start | bytes 4128776 | tf_op jit(solution)/shard_map/ppermute | solution.py:722
  68.6 31.0 %collective-permute-start.19 = (bf16[1024,512]{1,0:T(8,128)(2,1)}, bf16[1024,512]{1,0:T(8,128)(2,1)S(1)}, u32[]{:S(2)}, u32[]{:S(2)}) collective-permute-start(bf16[1024,512]{1,0:T(8,128)(2,1)} %get-tuple-element.66), channel_id=1, source_target_pairs={{0,1},{1,0},{2,3},{3,2},{4,5},{5,4},{6,7},{7,6},{8,9},{9,8},{10,11... | collective-permute-start | bytes 3145736 | tf_op jit(solution)/shard_map/ppermute | solution.py:722
  138.2 30.6 %collective-permute-start.20 = (bf16[256,768]{1,0:T(8,128)(2,1)S(1)}, bf16[256,768]{1,0:T(8,128)(2,1)S(1)}, u32[]{:S(2)}, u32[]{:S(2)}) collective-permute-start(bf16[256,768]{1,0:T(8,128)(2,1)S(1)} %slice.213), channel_id=1, source_target_pairs={{0,1},{1,0},{2,3},{3,2},{4,5},{5,4},{6,7},{7,6},{8,9},{9,8},{10,11... | collective-permute-start | bytes 1179656 | tf_op jit(solution)/shard_map/ppermute | solution.py:722
  158.9 24.1 %collective-permute-start.25 = (bf16[256,896]{1,0:T(8,128)(2,1)S(1)}, bf16[256,896]{1,0:T(8,128)(2,1)S(1)}, u32[]{:S(2)}, u32[]{:S(2)}) collective-permute-start(bf16[256,896]{1,0:T(8,128)(2,1)S(1)} %slice.224), channel_id=1, source_target_pairs={{0,1},{1,0},{2,3},{3,2},{4,5},{5,4},{6,7},{7,6},{8,9},{9,8},{10,11... | collective-permute-start | bytes 1376264 | tf_op jit(solution)/shard_map/ppermute | solution.py:722
  169.0 13.3 %collective-permute-start.21 = (bf16[128,768]{1,0:T(8,128)(2,1)S(1)}, bf16[128,768]{1,0:T(8,128)(2,1)S(1)}, u32[]{:S(2)}, u32[]{:S(2)}) collective-permute-start(bf16[128,768]{1,0:T(8,128)(2,1)S(1)} %slice.272), channel_id=1, source_target_pairs={{0,2},{1,3},{2,0},{3,1},{4,6},{5,7},{6,4},{7,5},{8,10},{9,11},{10,... | collective-permute-start | bytes 589832 | tf_op jit(solution)/shard_map/ppermute | solution.py:722
  181.4 23.6 %collective-permute-start.35 = (bf16[1024,512]{1,0:T(8,128)(2,1)S(1)}, bf16[1024,512]{1,0:T(8,128)(2,1)S(1)}, u32[]{:S(2)}, u32[]{:S(2)}) collective-permute-start(bf16[1024,512]{1,0:T(8,128)(2,1)S(1)} %slice.306), channel_id=1, source_target_pairs={{0,1},{1,0},{2,3},{3,2},{4,5},{5,4},{6,7},{7,6},{8,9},{9,8},{10,11... | collective-permute-start | bytes 3145736 | tf_op jit(solution)/shard_map/ppermute | solution.py:722
  181.9 24.1 %collective-permute-start.30 = (bf16[256,2688]{1,0:T(8,128)(2,1)S(1)}, bf16[256,2688]{1,0:T(8,128)(2,1)S(1)}, u32[]{:S(2)}, u32[]{:S(2)}) collective-permute-start(bf16[256,2688]{1,0:T(8,128)(2,1)S(1)} %slice.294), channel_id=1, source_target_pairs={{0,1},{1,0},{2,3},{3,2},{4,5},{5,4},{6,7},{7,6},{8,9},{9,8},{10,11... | collective-permute-start | bytes 4128776 | tf_op jit(solution)/shard_map/ppermute | solution.py:722
  183.1 7.7 %collective-permute-start.26 = (bf16[128,896]{1,0:T(8,128)(2,1)S(1)}, bf16[128,896]{1,0:T(8,128)(2,1)S(1)}, u32[]{:S(2)}, u32[]{:S(2)}) collective-permute-start(bf16[128,896]{1,0:T(8,128)(2,1)S(1)} %slice.281), channel_id=1, source_target_pairs={{0,2},{1,3},{2,0},{3,1},{4,6},{5,7},{6,4},{7,5},{8,10},{9,11},{10,... | collective-permute-start | bytes 688136 | tf_op jit(solution)/shard_map/ppermute | solution.py:722
  205.4 14.9 %collective-permute-start.36 = (bf16[512,512]{1,0:T(8,128)(2,1)S(1)}, bf16[512,512]{1,0:T(8,128)(2,1)S(1)}, u32[]{:S(2)}, u32[]{:S(2)}) collective-permute-start(bf16[512,512]{1,0:T(8,128)(2,1)S(1)} %slice.308), channel_id=1, source_target_pairs={{0,2},{1,3},{2,0},{3,1},{4,6},{5,7},{6,4},{7,5},{8,10},{9,11},{10,... | collective-permute-start | bytes 1572872 | tf_op jit(solution)/shard_map/ppermute | solution.py:722
  206.3 23.9 %collective-permute-start.31 = (bf16[128,2688]{1,0:T(8,128)(2,1)S(1)}, bf16[128,2688]{1,0:T(8,128)(2,1)S(1)}, u32[]{:S(2)}, u32[]{:S(2)}) collective-permute-start(bf16[128,2688]{1,0:T(8,128)(2,1)S(1)} %slice.296), channel_id=1, source_target_pairs={{0,2},{1,3},{2,0},{3,1},{4,6},{5,7},{6,4},{7,5},{8,10},{9,11},{10,... | collective-permute-start | bytes 2064392 | tf_op jit(solution)/shard_map/ppermute | solution.py:722
  220.5 11.4 %collective-permute-start.37 = (bf16[256,512]{1,0:T(8,128)(2,1)S(1)}, bf16[256,512]{1,0:T(8,128)(2,1)S(1)}, u32[]{:S(2)}, u32[]{:S(2)}) collective-permute-start(bf16[256,512]{1,0:T(8,128)(2,1)S(1)} %slice.310), channel_id=1, source_target_pairs={{0,4},{1,5},{2,6},{3,7},{4,0},{5,1},{6,2},{7,3},{8,12},{9,13},{10,... | collective-permute-start | bytes 786440 | tf_op jit(solution)/shard_map/ppermute | solution.py:722
  (32 other events, 286.0 us)
